TPU v7x, 32 devices: a whole 2x2x4 slice. The times are simulated.
32 devices in a mesh: groups: 2 (over y), seq: 4 (over z), inner: 2 (over x), head: 2 (over core).
Axes of the slice: x: 2, y: 2, z: 4, core: 2. Of those that a mesh axis runs over, the one named last changes fastest.
Arguments:
- queries: bfloat16 [2048, 32, 128], P(('groups', 'seq', 'inner'), 'head'), parts along dimension 0, as said below
- keys: bfloat16 [2048, 4, 128], P(('groups', 'seq', 'inner'), 'head'), parts along dimension 0
- values: bfloat16 [2048, 4, 128], P(('groups', 'seq', 'inner'), 'head'), parts along dimension 0, may hold values from -6 to 6
- log_decay: float32 [2048, 4], P(('groups', 'seq', 'inner'), 'head'), parts along dimension 0, as said below
- gain: float32 [32, 128], P('head'), may hold values from 0.1 to 1.9
- block_list: int32 [32, 16], P(('groups', 'seq', 'inner')), parts along dimension 0, may hold values from 0 to 15, as said below
Outputs:
- attended: bfloat16 [2048, 32, 128], P(('groups', 'seq', 'inner'), 'head'), parts along dimension 0
There are 2 independent parts, one for each index of `groups`. A program takes and returns all parts, laid end to end along the dimension named above; an argument that names none is the same for every part. Nothing has to cross between parts.
Inputs may be any that keep to these rules, and one draw needn't show every extreme that they name: Keys lie within -6 to 6; queries within -144 to 144. `log_decay`: each entry is below 0. `block_list`: entry 0 of row b is b. The sequence's pieces of 128 tokens fall into segments: piece p belongs to segment p modulo 2. Every entry of row b is a block at or before b in a piece of b's segment.
All inputs are finite; a program needn't handle non-finite values.
Results may differ from a plain program's by a relative error of at most 0.0017.
Values may be sent and summed in bfloat16 or wider, within the bound.
No kernel may reach another device: no remote copies, remote signals or barrier semaphores. Data moves between devices by JAX's collectives and lax.ppermute only.
A program may use at most 64 MiB of HBM per device.

v0:
```python
import jax
import jax.numpy as jnp
from jax import lax
from jax.sharding import PartitionSpec as P

BLK = 64
SEL = 16


HIGH = lax.Precision.HIGHEST


def prefix(shard, axis, combine, identity):
    devices, here = (lax.axis_size(axis), lax.axis_index(axis))
    everything = jax.tree.map(lambda part: lax.all_gather(part, axis), shard)
    start = jax.tree.map(
        lambda part, zero: jnp.broadcast_to(jnp.asarray(zero, part.dtype), part.shape),
        shard,
        identity,
    )

    def turn(k, before):
        reached = k < here
        new = combine(before, jax.tree.map(lambda part: part[k], everything))
        return jax.tree.map(lambda a, b: jnp.where(reached, a, b), new, before)

    return lax.fori_loop(0, devices, turn, start)


def combine(earlier, later):
    return (earlier[0] * later[0], later[0][:, None, None] * earlier[1] + later[1])


def shards(queries, keys, values, log_decay, gain, block_list):
    tokens, heads_loc, width = queries.shape
    kv_loc = keys.shape[1]
    rep = heads_loc // kv_loc
    qf = queries.astype(jnp.float32).reshape(tokens, kv_loc, rep, width)
    kf = keys.astype(jnp.float32)
    vf = values.astype(jnp.float32)
    cum = jnp.cumsum(log_decay, axis=0)
    total = cum[-1]
    causal = jnp.arange(tokens)[:, None] >= jnp.arange(tokens)[None, :]
    scores = jnp.einsum("tkrd,skd->krts", qf, kf, precision=HIGH)
    diff = cum.T[:, :, None] - cum.T[:, None, :]
    weight = jnp.where(causal[None], jnp.exp(jnp.minimum(diff, 0.0)), 0.0)
    intra = jnp.einsum("krts,skd->tkrd", scores * weight[:, None], vf, precision=HIGH)
    tail = jnp.exp(total[None, :] - cum)
    own_state = jnp.einsum("skd,ske->kde", kf * tail[:, :, None], vf, precision=HIGH)
    own_decay = jnp.exp(total)
    identity = (jnp.ones_like(own_decay), jnp.zeros_like(own_state))
    prior = prefix((own_decay, own_state), ("seq", "inner"), combine, identity)
    prior_state = prior[1]
    inter = jnp.exp(cum)[:, :, None, None] * jnp.einsum(
        "tkrd,kde->tkre", qf, prior_state, precision=HIGH
    )
    linear = (intra + inter).reshape(tokens, heads_loc, width)
    normed = (
        linear * lax.rsqrt(jnp.mean(linear * linear, axis=-1, keepdims=True) + 1e-06) * gain[None]
    )
    per_piece = tokens // BLK
    n_inner = lax.axis_size("inner")
    start_pos = (lax.axis_index("seq") * n_inner + lax.axis_index("inner")) * tokens
    seg_block = block_list // (n_inner * per_piece) * per_piece + block_list % per_piece
    seg_keys, seg_values = (
        lax.all_gather(keys, "seq", axis=0, tiled=True),
        lax.all_gather(values, "seq", axis=0, tiled=True),
    )
    key_blocks = seg_keys.reshape(-1, BLK, kv_loc, width)
    value_blocks = seg_values.reshape(-1, BLK, kv_loc, width)
    picked_keys = key_blocks[seg_block]
    picked_values = value_blocks[seg_block]
    lower = jnp.arange(SEL)[None, :] < jnp.arange(SEL)[:, None]
    repeat = jnp.any((block_list[:, :, None] == block_list[:, None, :]) & lower[None], axis=2)
    keep_all = jnp.logical_not(repeat)
    query_pos = start_pos + jnp.arange(tokens).reshape(per_piece, BLK)
    key_pos = block_list[:, :, None] * BLK + jnp.arange(BLK)[None, None, :]
    q_blocks = queries.reshape(per_piece, BLK, kv_loc, rep, width)

    def one_block(args):
        qblk, pk, pv, qpos, kpos, keep = args
        valid = keep[None, :, None] & (kpos[None] <= qpos[:, None, None])
        score = jnp.einsum(
            "qkrd,jukd->krqju", qblk, pk, preferred_element_type=jnp.float32
        ) * width ** (-0.5)
        score = jnp.where(valid[None, None], score, -1e30)
        top = jnp.max(score, axis=(3, 4), keepdims=True)
        expo = jnp.where(valid[None, None], jnp.exp(score - top), 0.0)
        denom = jnp.sum(expo, axis=(3, 4))
        weights = expo.astype(jnp.bfloat16)
        out = jnp.einsum("krqju,jukd->qkrd", weights, pv, preferred_element_type=jnp.float32)
        return out / jnp.transpose(denom, (2, 0, 1))[:, :, :, None]

    outs = lax.map(one_block, (q_blocks, picked_keys, picked_values, query_pos, key_pos, keep_all))
    sparse = outs.reshape(tokens, heads_loc, width)
    return (normed + sparse).astype(jnp.bfloat16)


def solution(mesh):
    return jax.shard_map(
        shards,
        mesh=mesh,
        in_specs=(
            P(("groups", "seq", "inner"), "head", None),
            P(("groups", "seq", "inner"), "head", None),
            P(("groups", "seq", "inner"), "head", None),
            P(("groups", "seq", "inner"), "head"),
            P("head", None),
            P(("groups", "seq", "inner"), None),
        ),
        out_specs=P(("groups", "seq", "inner"), "head", None),
        check_vma=False,
    )
```

profile of v0, /device:TPU:0, one launch (start us, length us, event | category | flops | bytes accessed | tf_op | source)
XLA Modules:
  0.0 109.4 jit_solution(16745564901405145584)
XLA Ops:
  6.5 0.8 copy.113
  7.3 0.2 reduce_window_sum.11
  7.5 0.6 slice_bitcast_fusion
  8.1 1.0 convert_multiply_fusion
  9.2 1.8 %fusion.30 = f32[2,128,128]{2,1,0:T(8,128)} fusion(f32[128,2,128]{2,1,0:T(2,128)S(1)} %convert_multiply_fusion, bf16[128,2,128]{2,1,0:T(2,128)(2,1)} %param.12), kind=kOutput, calls=%fused_computation.44 | convolution fusion | flops 50331648 | bytes 327680 | tf_op jit(solution)/shard_map/skd,ske->kde/dot_general | solution.py:49
  11.0 0.9 copy.121
  11.8 0.9 copy.129
  12.7 16.1 %all_gather.19 = bf16[512,2,128]{2,0,1:T(8,128)(2,1)S(1)} all-gather(bf16[128,2,128]{2,0,1:T(8,128)(2,1)S(1)} %copy.121), channel_id=1, replica_groups=mesh['groups'=2,'seq'=4,'inner'=2,'head'=2] {'seq'}, dimensions={0}, use_global_device_ids=true | all-gather | bytes 327680 | tf_op jit(solution)/shard_map/all_gather | solution.py:67
  28.8 0.7 broadcast_multiply_fusion
  29.6 0.9 and_reduce_fusion
  30.5 0.6 not.3
  31.2 0.6 add_add_fusion
  31.8 15.5 %all_gather.20 = bf16[512,2,128]{2,0,1:T(8,128)(2,1)S(1)} all-gather(bf16[128,2,128]{2,0,1:T(8,128)(2,1)S(1)} %copy.129), channel_id=1, replica_groups=mesh['groups'=2,'seq'=4,'inner'=2,'head'=2] {'seq'}, dimensions={0}, use_global_device_ids=true | all-gather | bytes 327680 | tf_op jit(solution)/shard_map/all_gather | solution.py:66
  47.3 0.7 gather_fusion
  48.0 0.9 gather_fusion.1
  48.9 18.8 %while.24 = (s32[]{:T(128)}, f32[2,64,2,8,128]{4,3,2,1,0:T(8,128)S(1)}, bf16[2,16,64,2,128]{4,2,3,1,0:T(8,128)(2,1)S(1)}, pred[2,16]{1,0:T(4,128)(4,1)}, s32[2,1...) while((s32[]{:T(128)}, ...), condition=%wide.region_8.9_spmd, body=%wide.region_5.8_spmd.sunk | while | flops 550762496 | bytes 18383788 | solution.py:94
  48.9 0.7 fusion.47
  49.6 0.7 fusion.48
  50.3 0.2 compare_and_fusion.2
  50.5 1.0 constant_dynamic-slice_fusion.7
  51.6 1.8 %fusion.49 = (f32[2,8,64]{2,1,0:T(8,128)S(1)}, f32[2,16,64,64,8]{3,2,4,1,0:T(8,128)S(1)}) fusion(pred[64,16,64]{0,2,1:T(8,128)(4,1)S(1)} %compare_and_fusion.2, bf16[1,64,2,8,128]{4,3,2,1,0:T(8,128)(2,1)S(1)} %constant_dynamic-slice_fusion.7, bf16[1,16,64,2,128]{4,2,3,1,0:T(8,128)(2,1)S(1)} %get-tuple-element.348), kind=kOutput, calls=%fused_computation.4.clone.1 | convolution fusion | flops 271580160 | bytes 5050368 | tf_op jit(solution)/shard_map/while/body/eval_jaxpr/qkrd,jukd->krqju/dot_general | solution.py:83
  53.4 2.3 %fusion.50 = f32[2,8,64]{2,1,0:T(8,128)S(1)} fusion(f32[2,16,64,64,8]{3,2,4,1,0:T(8,128)S(1)} %get-tuple-element.349, f32[2,8,64]{2,1,0:T(8,128)S(1)} %get-tuple-element.350, pred[64,16,64]{0,2,1:T(8,128)(4,1)S(1)} %compare_and_fusion.2), kind=kLoop, calls=%fused_computation.5.clone.1 | loop fusion | flops 5241856 | bytes 4268032 | tf_op jit(solution)/shard_map/while/body/eval_jaxpr/reduce_sum | solution.py:89
  55.7 2.3 %fusion.51 = f32[1,64,2,8,128]{4,1,3,2,0:T(8,128)S(1)} fusion(f32[2,16,64,64,8]{3,2,4,1,0:T(8,128)S(1)} %get-tuple-element.349, f32[2,8,64]{2,1,0:T(8,128)S(1)} %get-tuple-element.350, pred[64,16,64]{0,2,1:T(8,128)(4,1)S(1)} %compare_and_fusion.2, bf16[1,16,64,2,128]{4,2,3,1,0:T(8,128)(2,1)S(1)} %get-tuple-element.351, f32[64,2,8]{0,2,1:T(8,128)S(1)} %bitcast.148), kind=kOutput, calls=%fused_computation.11.clone.1 | convolution fusion | flops 273809408 | bytes 5316608 | tf_op jit(solution)/shard_map/while/body/eval_jaxpr/krqju,jukd->qkrd/dot_general | solution.py:91
  58.0 0.4 copy_dynamic-update-slice_fusion.2
  58.3 0.7 fusion.47
  59.0 0.7 fusion.48
  59.7 0.2 compare_and_fusion.2
  59.9 1.0 constant_dynamic-slice_fusion.7
  61.0 1.8 %fusion.49 = (f32[2,8,64]{2,1,0:T(8,128)S(1)}, f32[2,16,64,64,8]{3,2,4,1,0:T(8,128)S(1)}) fusion(pred[64,16,64]{0,2,1:T(8,128)(4,1)S(1)} %compare_and_fusion.2, bf16[1,64,2,8,128]{4,3,2,1,0:T(8,128)(2,1)S(1)} %constant_dynamic-slice_fusion.7, bf16[1,16,64,2,128]{4,2,3,1,0:T(8,128)(2,1)S(1)} %get-tuple-element.348), kind=kOutput, calls=%fused_computation.4.clone.1 | convolution fusion | flops 271580160 | bytes 5050368 | tf_op jit(solution)/shard_map/while/body/eval_jaxpr/qkrd,jukd->krqju/dot_general | solution.py:83
  62.8 2.3 %fusion.50 = f32[2,8,64]{2,1,0:T(8,128)S(1)} fusion(f32[2,16,64,64,8]{3,2,4,1,0:T(8,128)S(1)} %get-tuple-element.349, f32[2,8,64]{2,1,0:T(8,128)S(1)} %get-tuple-element.350, pred[64,16,64]{0,2,1:T(8,128)(4,1)S(1)} %compare_and_fusion.2), kind=kLoop, calls=%fused_computation.5.clone.1 | loop fusion | flops 5241856 | bytes 4268032 | tf_op jit(solution)/shard_map/while/body/eval_jaxpr/reduce_sum | solution.py:89
  65.0 2.3 %fusion.51 = f32[1,64,2,8,128]{4,1,3,2,0:T(8,128)S(1)} fusion(f32[2,16,64,64,8]{3,2,4,1,0:T(8,128)S(1)} %get-tuple-element.349, f32[2,8,64]{2,1,0:T(8,128)S(1)} %get-tuple-element.350, pred[64,16,64]{0,2,1:T(8,128)(4,1)S(1)} %compare_and_fusion.2, bf16[1,16,64,2,128]{4,2,3,1,0:T(8,128)(2,1)S(1)} %get-tuple-element.351, f32[64,2,8]{0,2,1:T(8,128)S(1)} %bitcast.148), kind=kOutput, calls=%fused_computation.11.clone.1 | convolution fusion | flops 273809408 | bytes 5316608 | tf_op jit(solution)/shard_map/while/body/eval_jaxpr/krqju,jukd->qkrd/dot_general | solution.py:91
  67.3 0.4 copy_dynamic-update-slice_fusion.2
  67.7 20.6 %all-gather.1 = f32[8,1,2]{2,1,0:T(1,128)S(1)} all-gather(f32[1,1,2]{2,1,0:T(1,128)S(1)} %copy-done.4), channel_id=1, replica_groups=mesh['groups'=2,'seq'=4,'inner'=2,'head'=2] {'seq','inner'}, dimensions={0}, use_global_device_ids=true | all-gather | bytes 72 | tf_op jit(solution)/shard_map/all_gather | solution.py:15
  88.5 0.1 exponential_select_fusion.1
  88.7 1.4 %fusion.26 = f32[2,8,128,128]{2,3,1,0:T(8,128)S(1)} fusion(f32[2,128,128]{1,2,0:T(8,128)S(1)} %exponential_select_fusion.1, bf16[128,2,8,128]{3,2,1,0:T(8,128)(2,1)} %bitcast.138, bf16[128,2,128,1]{2,1,0,3:T(2,128)(2,1)S(1)} %bitcast.144), kind=kOutput, calls=%fused_computation.38 | convolution fusion | flops 67371008 | bytes 1769472 | tf_op jit(solution)/shard_map/tkrd,skd->krts/dot_general | solution.py:44
  90.0 0.7 convolution_bitcast_fusion.2
  90.8 8.3 %while.25 = (s32[]{:T(128)}, f32[2,128,128]{2,1,0:T(8,128)S(1)}, s32[]{:T(128)}, f32[8,2]{1,0:T(8,128)S(1)}, f32[8,2,128,128]{3,2,1,0:T(8,128)}, /*index=5*/s32[]{:T(128)}, s32[]{:T(128)}) while((s32[]{:T(128)}, f32[2,128,128]{2,1,0:T(8,128)S(1)}, s32[]{:T(128)}, f32[8,2]{1,0:T(8,128)S(1)}, f32[8,2,128,128]{3,2,1,0:T(8,128)}, ...), condition=%wide.region_2.3_spmd.clone, body=%wide.region_1.2_spmd.clone.sunk | while | flops 131076 | bytes 393353 | solution.py:27
  90.8 1.0 fusion.52
  91.8 1.0 fusion.52
  92.9 1.0 fusion.52
  93.9 1.0 fusion.52
  94.9 1.0 fusion.52
  96.0 1.0 fusion.52
  97.0 1.0 fusion.52
  98.0 1.0 fusion.52
  99.0 1.8 %multiply_reduce_fusion = (f32[128,2,8]{0,2,1:T(8,128)S(1)}, f32[128,2,8,128]{0,3,2,1:T(8,128)S(1)}) fusion(f32[128,2,8,128]{0,3,2,1:T(8,128)S(1)} %convolution_bitcast_fusion.2, bf16[128,2,8,128]{3,2,1,0:T(8,128)(2,1)} %bitcast.139, f32[2,128,128]{2,1,0:T(8,128)S(1)} %get-tuple-element.141, f32[128,2]{0,1:T(2,128)S(1)} %copy.118), kind=kOutput, calls=%fused_computation.40 | convolution fusion | flops 403699712 | bytes 2761728 | tf_op jit(solution)/shard_map/tkrd,kde->tkre/dot_general | solution.py:54
  100.8 0.5 copy.126
  101.4 1.1 %add_convert_fusion = bf16[128,16,128]{2,1,0:T(8,128)(2,1)} fusion(f32[128,16,128]{2,1,0:T(8,128)S(1)} %bitcast.143, f32[128,16,128]{2,1,0:T(8,128)S(1)} %copy.126, f32[16,128]{1,0:T(8,128)S(1)} %copy-done.3, f32[128,16]{1,0:T(8,128)S(1)} %copy.125), kind=kLoop, calls=%fused_computation.39 | loop fusion | flops 1048576 | bytes 2637824 | tf_op jit(solution)/shard_map/convert_element_type | solution.py:96
  (39 shorter events, 0.8 us)
Async XLA Ops:
  6.5 84.2 %all-gather.4.cloned.1.call-start = ((), (), s32[]{:S(2)}) async-start(), calls=%async_computation | async-start | bytes 1179648 | tf_op jit(solution)/shard_map/all_gather | solution.py:15
  29.6 17.7 %copy-start.2 = (s32[1024]{0:T(1024)}, s32[1024]{0:T(1024)S(1)}, u32[]{:S(2)}) copy-start(s32[1024]{0:T(1024)S(1)} %pad_clamp_fusion) | copy-start | bytes 12292
  48.9 18.8 %copy-start.4 = (f32[1,1,2]{2,1,0:T(1,128)S(1)}, f32[1,1,2]{2,1,0:T(1,128)}, u32[]{:S(2)}) copy-start(f32[1,1,2]{2,1,0:T(1,128)} %get-tuple-element.264) | copy-start | bytes 28
  48.9 39.8 %copy-start = (bf16[128,2,128]{2,1,0:T(2,128)(2,1)S(1)}, bf16[128,2,128]{2,1,0:T(2,128)(2,1)}, u32[]{:S(2)}) copy-start(bf16[128,2,128]{2,1,0:T(2,128)(2,1)} %param.11) | copy-start | bytes 196612
  48.9 41.1 %copy-start.1 = (bf16[128,2,128]{2,1,0:T(2,128)(2,1)S(1)}, bf16[128,2,128]{2,1,0:T(2,128)(2,1)}, u32[]{:S(2)}) copy-start(bf16[128,2,128]{2,1,0:T(2,128)(2,1)} %param.12) | copy-start | bytes 196612
  67.7 33.7 %copy-start.3 = (f32[16,128]{1,0:T(8,128)S(1)}, f32[16,128]{1,0:T(8,128)}, u32[]{:S(2)}) copy-start(f32[16,128]{1,0:T(8,128)} %param.14) | copy-start | bytes 24580
Sparse Core Ops, SparseCore 0:
  11.1 43.4 all-gather.3
where the time goes:
time: 110 us; the launch traced here: 109 us
  blocking collectives  52.2 us (47%)
  other arithmetic  18.3 us (17%)
  matrix products  13.7 us (12%)
  between operations  13.6 us (12%)
  local copies, waits for them, and re-layouts  11.2 us (10%)
    all_gather x1, blocking collectives, prefix(): everything = jax.tree.map(lambda part: lax.all_gather(part, axis), shard)  20.6 us
    all_gather x1, blocking collectives, shards(): lax.all_gather(values, 'seq', axis=0, tiled=True)  16.1 us
    all_gather x1, blocking collectives, shards(): lax.all_gather(keys, 'seq', axis=0, tiled=True)  15.5 us
    select_n x8, other arithmetic, turn(): return jax.tree.map(lambda a, b: jnp.where(reached, a, b), new, before)  7.94 us
    dot_general x2, matrix products, one_block(): jnp.einsum('krqju,jukd->qkrd', weights, pv, preferred_element_type=jnp.fl...  4.6 us
    reduce_sum x2, other arithmetic, one_block(): denom = jnp.sum(expo, axis=(3, 4))  4.54 us
    dot_general x2, matrix products, one_block(): jnp.einsum('qkrd,jukd->krqju', qblk, pk, preferred_element_type=jnp.float32)  3.54 us
    unnamed x13, local copies, waits for them, and re-layouts  2.52 us
  transfers between devices with their start and end apart: 1, of which 0 were waited for; matrix products, arithmetic and copies ran while one was open for 25% of the time, Pallas kernels for 0%

commit v1 on v0

v1 whole, which is shorter than its diff:
```python
import functools

import jax
import jax.numpy as jnp
from jax import lax
from jax.experimental import pallas as pl
from jax.experimental.pallas import tpu as pltpu
from jax.sharding import PartitionSpec as P

BLK = 64
EXTRA = 16
HIGH = lax.Precision.HIGHEST
F32 = jnp.float32
BF16 = jnp.bfloat16
NT = (((1,), (1,)), ((), ()))
TN = (((0,), (0,)), ((), ()))
NEG = -1e30
VMEM = pl.BlockSpec(memory_space=pltpu.VMEM)
SMEM = pl.BlockSpec(memory_space=pltpu.SMEM)
PARAMS = pltpu.CompilerParams(vmem_limit_bytes=48 * 2**20)


def iota(shape, dim):
    return lax.broadcasted_iota(jnp.int32, shape, dim)


def mm(a, b, dims=(((1,), (0,)), ((), ())), precision=None):
    return lax.dot_general(a, b, dims, preferred_element_type=F32, precision=precision)


def halves(x):
    hi = x.astype(BF16)
    return hi, (x - hi.astype(F32)).astype(BF16)


def pack_kernel(kv, keys, values, decay, out, even):
    tokens = keys.shape[0] // kv
    for n, ref in enumerate((keys, values)):
        even[...] = ref[...].astype(F32)
        for g in range(kv):
            at = (n * kv + g) * tokens
            out[at : at + tokens, :] = even[pl.ds(g, tokens, stride=kv), :].astype(BF16)
    left = jnp.maximum(decay[...], NEG)
    parts = []
    for _ in range(3):
        parts.append(left.astype(BF16).astype(F32))
        left = left - parts[-1]
    rest = jnp.zeros((EXTRA - 3 * kv, tokens), F32)
    out[2 * kv * tokens :, :] = jnp.concatenate([*parts, rest], axis=0).astype(BF16)


def decays(piece, kv):
    rows = piece[piece.shape[0] - EXTRA :, :].astype(F32)
    return rows[:kv] + rows[kv : 2 * kv] + rows[2 * kv : 3 * kv]


def local_kernel(kv, queries, piece, q_out, lin_out):
    tokens, heads, width = queries.shape
    rep = heads // kv
    rows = tokens * rep
    qf = queries[...].astype(F32)
    dec = decays(piece, kv)
    upto = (iota((rows, tokens), 1) <= iota((rows, tokens), 0) // rep).astype(F32)
    dec8 = jnp.concatenate([dec, jnp.zeros((8 - kv, tokens), F32)], axis=0)
    ahead = (iota((tokens, tokens), 0) <= iota((tokens, tokens), 1)).astype(F32)
    cum_row = mm(dec8, ahead, precision=HIGH)
    cum_col = mm(upto, dec8, NT, precision=HIGH)
    for g in range(kv):
        q = qf[:, g * rep : (g + 1) * rep, :].reshape(rows, width).astype(BF16)
        q_out[g] = q
        k = piece[g * tokens : (g + 1) * tokens, :]
        v = piece[(kv + g) * tokens : (kv + g + 1) * tokens, :]
        diff = cum_col[:, g : g + 1] - cum_row[g : g + 1, :]
        weight = jnp.where(upto > 0, jnp.exp(jnp.minimum(diff, 0.0)), 0.0)
        hi, lo = halves(mm(q, k, NT) * weight)
        lin_out[g] = mm(hi, v) + mm(lo, v)


def sparse_kernel(kv, slots, ids, n_mine, queries, blocks, *refs):
    pieces, out, scores = refs[:n_mine], refs[-2], refs[-1]
    _, rows, width = queries.shape
    per = blocks.shape[0]
    tokens = per * BLK
    rep = rows // tokens
    here, number = ids()
    factor = width**-0.5 * 1.4426950408889634
    part = rows // per

    def piece_of(i):
        return pieces[i] if n_mine > 1 else pieces[0].at[i]

    lane = iota((1, tokens), 1)
    for b in range(per):
        biases = []
        for i in range(slots):
            block = number(i) * per + lane // BLK
            listed = block == blocks[b, 0]
            for j in range(1, blocks.shape[1]):
                listed = jnp.logical_or(listed, block == blocks[b, j])
            biases.append(jnp.where(listed, 0.0, NEG))
        row = b * BLK + iota((part, tokens), 0) // rep
        position = here * tokens + row
        for g in range(kv):
            q = queries[g, b * part : (b + 1) * part, :]
            top = None
            for i in range(slots):
                k = piece_of(i)[g * tokens : (g + 1) * tokens, :]
                s = mm(q, k, NT) + biases[i]
                if n_mine == 1 or i == 0:
                    s = jnp.where(number(i) * tokens + iota((part, tokens), 1) <= position, s, NEG)
                scores[:, i * tokens : (i + 1) * tokens] = s
                top = s if top is None else jnp.maximum(top, s)
            top = jnp.max(top, axis=1, keepdims=True)
            total, acc = None, None
            for i in range(slots):
                v = piece_of(i)[(kv + g) * tokens : (kv + g + 1) * tokens, :]
                e = jnp.exp2((scores[:, i * tokens : (i + 1) * tokens] - top) * factor)
                o = mm(e.astype(BF16), v)
                total = e if total is None else total + e
                acc = o if acc is None else acc + o
            denom = jnp.sum(total, axis=1, keepdims=True)
            out[g, b * part : (b + 1) * part, :] = acc / denom


def final_kernel(kv, slots, distance, n_mine, queries, lin, sparse, gain, own, *refs):
    pieces, out = refs[:n_mine], refs[-1]
    _, rows, width = queries.shape
    tokens, heads, _ = out.shape
    rep = heads // kv
    after = (iota((tokens, tokens), 1) > iota((tokens, tokens), 0)).astype(F32)

    def terms(piece, dec, shift, keep, state):
        suffix = mm(after, dec, NT, precision=HIGH)
        result = []
        for g in range(kv):
            w = jnp.exp(jnp.minimum(suffix[:, g : g + 1] + shift[g], 0.0))
            w = jnp.where(keep, w, 0.0)
            k = piece[g * tokens : (g + 1) * tokens, :]
            v = piece[(kv + g) * tokens : (kv + g + 1) * tokens, :].astype(F32) * w
            hi, lo = halves(v)
            result.append(state[g] + mm(k, hi, TN) + mm(k, lo, TN))
        return result

    def padded(piece):
        return jnp.concatenate([decays(piece, kv), jnp.zeros((8 - kv, tokens), F32)], axis=0)

    state = [jnp.zeros((width, width), F32) for _ in range(kv)]
    if n_mine > 1:
        decs = [padded(p) for p in pieces]
        totals = [jnp.sum(d, axis=1, keepdims=True) for d in decs]
        where = [distance(i) for i in range(slots)]
        for i in range(slots):
            shift = jnp.zeros((8, 1), F32)
            for j in range(slots):
                if j != i:
                    between = jnp.logical_and(where[j] >= 1, where[j] < where[i])
                    shift = shift + jnp.where(between, totals[j], 0.0)
            keep = distance(i, True)
            shifts = [shift[g : g + 1, :] for g in range(kv)]
            state = terms(pieces[i], decs[i], shifts, keep, state)
    else:

        def turn(n, carry):
            shift, state = carry
            at, keep = distance(n)
            piece = pieces[0].at[at]
            dec = padded(piece)
            state = terms(piece, dec, [shift[g : g + 1, :] for g in range(kv)], keep, state)
            total = jnp.sum(dec, axis=1, keepdims=True)
            return shift + jnp.where(keep, total, 0.0), tuple(state)

        _, state = lax.fori_loop(0, slots, turn, (jnp.zeros((8, 1), F32), tuple(state)))
    upto = (iota((rows, tokens), 1) <= iota((rows, tokens), 0) // rep).astype(F32)
    cum = mm(upto, padded(own), NT, precision=HIGH)
    both = []
    for g in range(kv):
        q = queries[g]
        hi, lo = halves(state[g])
        inter = mm(q, hi) + mm(q, lo)
        linear = lin[g] + jnp.exp(cum[:, g : g + 1]) * inter
        mean = jnp.mean(linear * linear, axis=1, keepdims=True)
        normed = (linear * lax.rsqrt(mean + 1e-06)).reshape(tokens, rep, width)
        normed = normed * gain[g * rep : (g + 1) * rep, :][None]
        both.append(normed + sparse[g].reshape(tokens, rep, width))
    out[...] = jnp.concatenate(both, axis=1).astype(BF16)


def shards(queries, keys, values, log_decay, gain, block_list):
    tokens, heads, width = queries.shape
    kv = keys.shape[1]
    rep = heads // kv
    rows = tokens * rep
    n_seq, n_inner = lax.axis_size("seq"), lax.axis_size("inner")
    shape = jax.ShapeDtypeStruct
    piece = pl.pallas_call(
        functools.partial(pack_kernel, kv),
        out_shape=shape((2 * kv * tokens + EXTRA, width), BF16),
        in_specs=[VMEM] * 3,
        out_specs=VMEM,
        scratch_shapes=[pltpu.VMEM((tokens * kv, width), F32)],
        compiler_params=PARAMS,
    )(keys.reshape(-1, width), values.reshape(-1, width), log_decay.T)
    q, lin = pl.pallas_call(
        functools.partial(local_kernel, kv),
        out_shape=(shape((kv, rows, width), BF16), shape((kv, rows, width), F32)),
        in_specs=[VMEM] * 2,
        out_specs=(VMEM, VMEM),
        compiler_params=PARAMS,
    )(queries, piece)

    few = n_seq == 4 and n_inner == 2
    if few:
        def forward(x, s):
            return lax.ppermute(x, "seq", [(i, i + s) for i in range(n_seq - s)])

        moved = {s: forward(piece, s) for s in range(n_seq - 1, 0, -1)}
        column = [piece, *(moved[s] for s in range(1, n_seq))]
        other = [lax.ppermute(x, "inner", [(0, 1), (1, 0)]) for x in column]

        def ids():
            z, x = lax.axis_index("seq"), lax.axis_index("inner")
            return z * n_inner + x, lambda i: (z - i) * n_inner + x

        def distance(i, keep=False):
            z, x = lax.axis_index("seq"), lax.axis_index("inner")
            if i < n_seq - 1:
                back, far = i + 1, (i + 1) * n_inner
            else:
                back = i - (n_seq - 1)
                far = back * n_inner + jnp.where(x == 0, -1, 1)
            return jnp.logical_and(far >= 1, back <= z) if keep else far

        sparse_in, final_in = column, column[1:] + other
        slots, n_all = n_seq, 2 * n_seq - 1
    else:
        column = lax.all_gather(piece, "seq")
        everything = lax.all_gather(column, "inner").reshape(n_inner * n_seq, *piece.shape)

        def ids():
            z, x = lax.axis_index("seq"), lax.axis_index("inner")
            return z * n_inner + x, lambda i: i * n_inner + x

        def distance(n):
            here = lax.axis_index("seq") * n_inner + lax.axis_index("inner")
            p = n_seq * n_inner - 1 - n
            return lax.rem(p, n_inner) * n_seq + lax.div(p, n_inner), p < here

        sparse_in, final_in = [column], [everything]
        slots, n_all = n_seq, n_seq * n_inner

    per = tokens // BLK
    sparse = pl.pallas_call(
        functools.partial(sparse_kernel, kv, slots, ids, len(sparse_in)),
        out_shape=shape((kv, rows, width), F32),
        in_specs=[VMEM, SMEM] + [VMEM] * len(sparse_in),
        out_specs=VMEM,
        scratch_shapes=[pltpu.VMEM((rows // per, slots * tokens), F32)],
        compiler_params=PARAMS,
    )(q, block_list, *sparse_in)
    return pl.pallas_call(
        functools.partial(final_kernel, kv, n_all, distance, len(final_in)),
        out_shape=shape((tokens, heads, width), BF16),
        in_specs=[VMEM] * (5 + len(final_in)),
        out_specs=VMEM,
        compiler_params=PARAMS,
    )(q, lin, sparse, gain, piece, *final_in)


def solution(mesh):
    tokens = P(("groups", "seq", "inner"), "head", None)
    return jax.shard_map(
        shards,
        mesh=mesh,
        in_specs=(
            tokens,
            tokens,
            tokens,
            P(("groups", "seq", "inner"), "head"),
            P("head", None),
            P(("groups", "seq", "inner"), None),
        ),
        out_specs=tokens,
        check_vma=False,
    )
```

time: 110 us -> 32.3 us (0.29)
  the two profiles are of different devices: /device:TPU:0 before, /device:TPU:16 now
where the time goes in v1:
time: 32.3 us; the launch traced here: 31.9 us
  starting transfers between devices  11.1 us (34%)
  Pallas kernels  8.49 us (26%)
  waiting for transfers between devices  8.15 us (25%)
  local copies, waits for them, and re-layouts  4.08 us (13%)
    ppermute x3, waiting for transfers between devices, forward(): return lax.ppermute(x, 'seq', [(i, i + s) for i in range(n_seq - s)])  8.14 us
    ppermute x3, starting transfers between devices, forward(): return lax.ppermute(x, 'seq', [(i, i + s) for i in range(n_seq - s)])  6.07 us
    ppermute x4, starting transfers between devices, shards(): other = [lax.ppermute(x, 'inner', [(0, 1), (1, 0)]) for x in column]  5.07 us
    pallas_call x1, Pallas kernels, shards(): pl.pallas_call(functools.partial(final_kernel, kv, n_all, distance, len(f...  4.13 us
    unnamed x12, local copies, waits for them, and re-layouts  4.08 us
    pallas_call x1, Pallas kernels, shards(): pl.pallas_call(functools.partial(sparse_kernel, kv, slots, ids, len(spars...  2.59 us
    pallas_call x1, Pallas kernels, shards(): pl.pallas_call(functools.partial(local_kernel, kv), out_shape=(shape((kv,...  1.72 us
  transfers between devices with their start and end apart: 7, of which 2 were waited for; matrix products, arithmetic and copies ran while one was open for 0% of the time, Pallas kernels for 14%

profile of v1, /device:TPU:16, one launch (start us, length us, event | category | flops | bytes accessed | tf_op | source)
XLA Modules:
  0.0 31.9 jit_solution(9346823496008275819)
XLA Ops:
  0.0 0.0 copy-start.4
  0.0 0.7 %copy-done.4 = f32[128,2]{0,1:T(2,128)S(1)} copy-done((f32[128,2]{0,1:T(2,128)S(1)}, f32[128,2]{0,1:T(2,128)}, u32[]{:S(2)}) %copy-start.4) | copy-done | bytes 1048
  0.7 0.0 copy-start.1
  0.7 0.8 %copy-done.1 = bf16[128,2,128]{2,1,0:T(2,128)(2,1)S(1)} copy-done((bf16[128,2,128]{2,1,0:T(2,128)(2,1)S(1)}, bf16[128,2,128]{2,1,0:T(2,128)(2,1)}, u32[]{:S(2)}) %copy-start.1) | copy-done | bytes 65560
  1.5 0.0 copy-start.2
  1.5 0.8 %copy-done.2 = bf16[128,2,128]{2,1,0:T(2,128)(2,1)S(1)} copy-done((bf16[128,2,128]{2,1,0:T(2,128)(2,1)S(1)}, bf16[128,2,128]{2,1,0:T(2,128)(2,1)}, u32[]{:S(2)}) %copy-start.2) | copy-done | bytes 65560
  2.4 0.7 %collective-permute-start.2 = (bf16[528,128]{1,0:T(8,128)(2,1)S(1)}, bf16[528,128]{1,0:T(8,128)(2,1)S(1)}, u32[]{:S(2)}, u32[]{:S(2)}) collective-permute-start(bf16[528,128]{1,0:T(8,128)(2,1)S(1)} %shard_map.64.piece.refs_0_.own), channel_id=1, source_target_pairs={{0,12},{1,13},{2,14},{3,15},{16,28},{17,29},{18,30},{19,31}} | collective-permute-start | bytes 405512 | tf_op jit(solution)/shard_map/ppermute | solution.py:214
  3.1 1.3 %collective-permute-start.1 = (bf16[528,128]{1,0:T(8,128)(2,1)S(1)}, bf16[528,128]{1,0:T(8,128)(2,1)S(1)}, u32[]{:S(2)}, u32[]{:S(2)}) collective-permute-start(bf16[528,128]{1,0:T(8,128)(2,1)S(1)} %shard_map.64.piece.refs_0_.own), channel_id=1, source_target_pairs={{0,8},{4,12},{1,9},{5,13},{2,10},{6,14},{3,11},{7,15},{16,24},{20,... | collective-permute-start | bytes 405512 | tf_op jit(solution)/shard_map/ppermute | solution.py:214
  4.4 4.1 %collective-permute-start = (bf16[528,128]{1,0:T(8,128)(2,1)S(1)}, bf16[528,128]{1,0:T(8,128)(2,1)S(1)}, u32[]{:S(2)}, u32[]{:S(2)}) collective-permute-start(bf16[528,128]{1,0:T(8,128)(2,1)S(1)} %shard_map.64.piece.refs_0_.own), channel_id=1, source_target_pairs={{0,4},{4,8},{8,12},{1,5},{5,9},{9,13},{2,6},{6,10},{10,14},{3,7},{... | collective-permute-start | bytes 405512 | tf_op jit(solution)/shard_map/ppermute | solution.py:214
  8.5 1.6 %collective-permute-start.3 = (bf16[528,128]{1,0:T(8,128)(2,1)S(1)}, bf16[528,128]{1,0:T(8,128)(2,1)S(1)}, u32[]{:S(2)}, u32[]{:S(2)}) collective-permute-start(bf16[528,128]{1,0:T(8,128)(2,1)S(1)} %shard_map.64.piece.refs_0_.own), channel_id=1, source_target_pairs={{0,2},{2,0},{1,3},{3,1},{4,6},{6,4},{5,7},{7,5},{8,10},{10,8},{9,1... | collective-permute-start | bytes 405512 | tf_op jit(solution)/shard_map/ppermute | solution.py:218
  10.1 0.0 collective-permute-done.2.refs_3_.refs_2_
  10.1 0.5 %collective-permute-start.6 = (bf16[528,128]{1,0:T(8,128)(2,1)S(1)}, bf16[528,128]{1,0:T(8,128)(2,1)S(1)}, u32[]{:S(2)}, u32[]{:S(2)}) collective-permute-start(bf16[528,128]{1,0:T(8,128)(2,1)S(1)} %collective-permute-done.2.refs_3_.refs_2_), channel_id=1, source_target_pairs={{0,2},{2,0},{1,3},{3,1},{4,6},{6,4},{5,7},{7,5},{8,10},{10,8},{9,1... | collective-permute-start | bytes 405512 | tf_op jit(solution)/shard_map/ppermute | solution.py:218
  10.6 5.0 %collective-permute-done.1.refs_2_.refs_1_ = bf16[528,128]{1,0:T(8,128)(2,1)S(1)} collective-permute-done((bf16[528,128]{1,0:T(8,128)(2,1)S(1)}, bf16[528,128]{1,0:T(8,128)(2,1)S(1)}, u32[]{:S(2)}, u32[]{:S(2)}) %collective-permute-start.1) | collective-permute-done | bytes 135200 | tf_op jit(solution)/shard_map/ppermute | solution.py:214
  15.6 1.5 %collective-permute-start.5 = (bf16[528,128]{1,0:T(8,128)(2,1)S(1)}, bf16[528,128]{1,0:T(8,128)(2,1)S(1)}, u32[]{:S(2)}, u32[]{:S(2)}) collective-permute-start(bf16[528,128]{1,0:T(8,128)(2,1)S(1)} %collective-permute-done.1.refs_2_.refs_1_), channel_id=1, source_target_pairs={{0,2},{2,0},{1,3},{3,1},{4,6},{6,4},{5,7},{7,5},{8,10},{10,8},{9,1... | collective-permute-start | bytes 405512 | tf_op jit(solution)/shard_map/ppermute | solution.py:218
  17.1 3.1 %collective-permute-done.refs_1_.refs_0_ = bf16[528,128]{1,0:T(8,128)(2,1)S(1)} collective-permute-done((bf16[528,128]{1,0:T(8,128)(2,1)S(1)}, bf16[528,128]{1,0:T(8,128)(2,1)S(1)}, u32[]{:S(2)}, u32[]{:S(2)}) %collective-permute-start) | collective-permute-done | bytes 135200 | tf_op jit(solution)/shard_map/ppermute | solution.py:214
  20.2 1.5 %collective-permute-start.4 = (bf16[528,128]{1,0:T(8,128)(2,1)S(1)}, bf16[528,128]{1,0:T(8,128)(2,1)S(1)}, u32[]{:S(2)}, u32[]{:S(2)}) collective-permute-start(bf16[528,128]{1,0:T(8,128)(2,1)S(1)} %collective-permute-done.refs_1_.refs_0_), channel_id=1, source_target_pairs={{0,2},{2,0},{1,3},{3,1},{4,6},{6,4},{5,7},{7,5},{8,10},{10,8},{9,1... | collective-permute-start | bytes 405512 | tf_op jit(solution)/shard_map/ppermute | solution.py:218
  21.7 0.0 copy-start
  21.7 1.0 %copy-done = bf16[128,16,128]{2,1,0:T(8,128)(2,1)S(1)} copy-done((bf16[128,16,128]{2,1,0:T(8,128)(2,1)S(1)}, bf16[128,16,128]{2,1,0:T(8,128)(2,1)}, u32[]{:S(2)}) %copy-start) | copy-done | bytes 524312
  22.8 1.7 %shard_map.65 = (bf16[2,1024,128]{2,1,0:T(8,128)(2,1)S(1)}, f32[2,1024,128]{2,1,0:T(8,128)S(1)}) custom-call(bf16[128,16,128]{2,1,0:T(8,128)(2,1)S(1)} %copy-done, bf16[528,128]{1,0:T(8,128)(2,1)S(1)} %shard_map.64.piece.refs_0_.own), custom_call_target="tpu_custom_call" | custom-call | tf_op jit(solution)/shard_map/pallas_call | solution.py:203
  24.5 0.0 copy-start.5
  24.5 0.7 %copy-done.5 = s32[2,16]{1,0:T(2,128)S(1)} copy-done((s32[2,16]{1,0:T(2,128)S(1)}, s32[2,16]{1,0:T(2,128)}, u32[]{:S(2)}) %copy-start.5) | copy-done | bytes 152
  25.2 0.0 copy-start.3
  25.2 2.6 %shard_map.66.sparse = f32[2,1024,128]{2,1,0:T(8,128)S(1)} custom-call(bf16[2,1024,128]{2,1,0:T(8,128)(2,1)S(1)} %get-tuple-element.7.queries, s32[2,16]{1,0:T(2,128)S(1)} %copy-done.5, bf16[528,128]{1,0:T(8,128)(2,1)S(1)} %shard_map.64.piece.refs_0_.own, bf16[528,128]{1,0:T(8,128)(2,1)S(1)} %collective-permute-done.refs_1_.refs_0_, ...), custom_call_target="tpu_custom_call" | custom-call | tf_op jit(solution)/shard_map/pallas_call | solution.py:252
  27.8 0.0 collective-permute-done.3.refs_3_
  27.8 0.0 collective-permute-done.6.refs_6_
  27.8 0.0 collective-permute-done.5.refs_5_
  27.8 0.0 collective-permute-done.4.refs_4_
  27.8 0.0 copy-done.3
  27.8 4.1 %shard_map.67 = bf16[128,16,128]{2,1,0:T(8,128)(2,1)} custom-call(bf16[2,1024,128]{2,1,0:T(8,128)(2,1)S(1)} %get-tuple-element.7.queries, f32[2,1024,128]{2,1,0:T(8,128)S(1)} %get-tuple-element.8.lin, f32[2,1024,128]{2,1,0:T(8,128)S(1)} %shard_map.66.sparse, f32[16,128]{1,0:T(8,128)S(1)} %copy-done.3, bf16[528,128]{1,0:T(8,128)(2,1)S(1)} %shard_map.64.piece.refs_0_.own, ...), custom_call_target="tpu_custom_call" | custom-call | tf_op jit(solution)/shard_map/pallas_call | solution.py:260
  (1 shorter events, 0.0 us)
Async XLA Ops:
  0.0 0.7 %copy-start.4 = (f32[128,2]{0,1:T(2,128)S(1)}, f32[128,2]{0,1:T(2,128)}, u32[]{:S(2)}) copy-start(f32[128,2]{0,1:T(2,128)} %param.9) | copy-start | bytes 3076
  0.7 0.8 %copy-start.1 = (bf16[128,2,128]{2,1,0:T(2,128)(2,1)S(1)}, bf16[128,2,128]{2,1,0:T(2,128)(2,1)}, u32[]{:S(2)}) copy-start(bf16[128,2,128]{2,1,0:T(2,128)(2,1)} %param.7) | copy-start | bytes 196612
  1.5 0.8 %copy-start.2 = (bf16[128,2,128]{2,1,0:T(2,128)(2,1)S(1)}, bf16[128,2,128]{2,1,0:T(2,128)(2,1)}, u32[]{:S(2)}) copy-start(bf16[128,2,128]{2,1,0:T(2,128)(2,1)} %param.8) | copy-start | bytes 196612
  2.4 7.7 %collective-permute-start.2 = (bf16[528,128]{1,0:T(8,128)(2,1)S(1)}, bf16[528,128]{1,0:T(8,128)(2,1)S(1)}, u32[]{:S(2)}, u32[]{:S(2)}) collective-permute-start(bf16[528,128]{1,0:T(8,128)(2,1)S(1)} %shard_map.64.piece.refs_0_.own), channel_id=1, source_target_pairs={{0,12},{1,13},{2,14},{3,15},{16,28},{17,29},{18,30},{19,31}} | collective-permute-start | bytes 405512 | tf_op jit(solution)/shard_map/ppermute | solution.py:214
  3.1 12.5 %collective-permute-start.1 = (bf16[528,128]{1,0:T(8,128)(2,1)S(1)}, bf16[528,128]{1,0:T(8,128)(2,1)S(1)}, u32[]{:S(2)}, u32[]{:S(2)}) collective-permute-start(bf16[528,128]{1,0:T(8,128)(2,1)S(1)} %shard_map.64.piece.refs_0_.own), channel_id=1, source_target_pairs={{0,8},{4,12},{1,9},{5,13},{2,10},{6,14},{3,11},{7,15},{16,24},{20,... | collective-permute-start | bytes 405512 | tf_op jit(solution)/shard_map/ppermute | solution.py:214
  4.4 15.8 %collective-permute-start = (bf16[528,128]{1,0:T(8,128)(2,1)S(1)}, bf16[528,128]{1,0:T(8,128)(2,1)S(1)}, u32[]{:S(2)}, u32[]{:S(2)}) collective-permute-start(bf16[528,128]{1,0:T(8,128)(2,1)S(1)} %shard_map.64.piece.refs_0_.own), channel_id=1, source_target_pairs={{0,4},{4,8},{8,12},{1,5},{5,9},{9,13},{2,6},{6,10},{10,14},{3,7},{... | collective-permute-start | bytes 405512 | tf_op jit(solution)/shard_map/ppermute | solution.py:214
  8.5 19.3 %collective-permute-start.3 = (bf16[528,128]{1,0:T(8,128)(2,1)S(1)}, bf16[528,128]{1,0:T(8,128)(2,1)S(1)}, u32[]{:S(2)}, u32[]{:S(2)}) collective-permute-start(bf16[528,128]{1,0:T(8,128)(2,1)S(1)} %shard_map.64.piece.refs_0_.own), channel_id=1, source_target_pairs={{0,2},{2,0},{1,3},{3,1},{4,6},{6,4},{5,7},{7,5},{8,10},{10,8},{9,1... | collective-permute-start | bytes 405512 | tf_op jit(solution)/shard_map/ppermute | solution.py:218
  10.1 17.7 %collective-permute-start.6 = (bf16[528,128]{1,0:T(8,128)(2,1)S(1)}, bf16[528,128]{1,0:T(8,128)(2,1)S(1)}, u32[]{:S(2)}, u32[]{:S(2)}) collective-permute-start(bf16[528,128]{1,0:T(8,128)(2,1)S(1)} %collective-permute-done.2.refs_3_.refs_2_), channel_id=1, source_target_pairs={{0,2},{2,0},{1,3},{3,1},{4,6},{6,4},{5,7},{7,5},{8,10},{10,8},{9,1... | collective-permute-start | bytes 405512 | tf_op jit(solution)/shard_map/ppermute | solution.py:218
  15.6 12.2 %collective-permute-start.5 = (bf16[528,128]{1,0:T(8,128)(2,1)S(1)}, bf16[528,128]{1,0:T(8,128)(2,1)S(1)}, u32[]{:S(2)}, u32[]{:S(2)}) collective-permute-start(bf16[528,128]{1,0:T(8,128)(2,1)S(1)} %collective-permute-done.1.refs_2_.refs_1_), channel_id=1, source_target_pairs={{0,2},{2,0},{1,3},{3,1},{4,6},{6,4},{5,7},{7,5},{8,10},{10,8},{9,1... | collective-permute-start | bytes 405512 | tf_op jit(solution)/shard_map/ppermute | solution.py:218
  20.2 7.6 %collective-permute-start.4 = (bf16[528,128]{1,0:T(8,128)(2,1)S(1)}, bf16[528,128]{1,0:T(8,128)(2,1)S(1)}, u32[]{:S(2)}, u32[]{:S(2)}) collective-permute-start(bf16[528,128]{1,0:T(8,128)(2,1)S(1)} %collective-permute-done.refs_1_.refs_0_), channel_id=1, source_target_pairs={{0,2},{2,0},{1,3},{3,1},{4,6},{6,4},{5,7},{7,5},{8,10},{10,8},{9,1... | collective-permute-start | bytes 405512 | tf_op jit(solution)/shard_map/ppermute | solution.py:218
  21.7 1.0 %copy-start = (bf16[128,16,128]{2,1,0:T(8,128)(2,1)S(1)}, bf16[128,16,128]{2,1,0:T(8,128)(2,1)}, u32[]{:S(2)}) copy-start(bf16[128,16,128]{2,1,0:T(8,128)(2,1)} %queries.1) | copy-start | bytes 1572868
  24.5 0.7 %copy-start.5 = (s32[2,16]{1,0:T(2,128)S(1)}, s32[2,16]{1,0:T(2,128)}, u32[]{:S(2)}) copy-start(s32[2,16]{1,0:T(2,128)} %blocks.1) | copy-start | bytes 388
  25.2 2.6 %copy-start.3 = (f32[16,128]{1,0:T(8,128)S(1)}, f32[16,128]{1,0:T(8,128)}, u32[]{:S(2)}) copy-start(f32[16,128]{1,0:T(8,128)} %gain.1) | copy-start | bytes 24580

commit v2 on v0

v2 whole, which is shorter than its diff:
```python
import functools

import jax
import jax.numpy as jnp
from jax import lax
from jax.experimental import pallas as pl
from jax.experimental.pallas import tpu as pltpu
from jax.sharding import PartitionSpec as P

BLK = 64
EXTRA = 16
F32 = jnp.float32
BF16 = jnp.bfloat16
NT = (((1,), (1,)), ((), ()))
TN = (((0,), (0,)), ((), ()))
NEG = -1e30
NEVER = 1 << 20
VMEM = pl.BlockSpec(memory_space=pltpu.VMEM)
HBM = pl.BlockSpec(memory_space=pltpu.HBM)
SMEM = pl.BlockSpec(memory_space=pltpu.SMEM)
PARAMS = pltpu.CompilerParams(vmem_limit_bytes=48 * 2**20)


def iota(shape, dim):
    return lax.broadcasted_iota(jnp.int32, shape, dim)


def mm(a, b, dims=(((1,), (0,)), ((), ()))):
    return lax.dot_general(a, b, dims, preferred_element_type=F32)


def halves(x):
    hi = x.astype(BF16)
    return hi, (x - hi.astype(F32)).astype(BF16)


def pack_kernel(kv, keys, values, decay, out, kv_in, decay_in, even, sems):
    tokens = keys.shape[0] // kv
    copies = [
        pltpu.make_async_copy(keys, kv_in.at[0], sems.at[0]),
        pltpu.make_async_copy(values, kv_in.at[1], sems.at[1]),
        pltpu.make_async_copy(decay, decay_in, sems.at[2]),
    ]
    for c in copies:
        c.start()
    for n in range(2):
        copies[n].wait()
        even[...] = kv_in[n].astype(F32)
        for g in range(kv):
            at = (n * kv + g) * tokens
            out[at : at + tokens, :] = even[pl.ds(g, tokens, stride=kv), :].astype(BF16)
    copies[2].wait()
    left = jnp.maximum(decay_in[...], NEG)
    parts = []
    for _ in range(3):
        parts.append(left.astype(BF16).astype(F32))
        left = left - parts[-1]
    rest = jnp.zeros((EXTRA - 3 * kv, tokens), F32)
    out[2 * kv * tokens :, :] = jnp.concatenate([*parts, rest], axis=0).astype(BF16)


def parts_of(piece, kv):
    rows = piece[piece.shape[0] - EXTRA :, :].astype(F32)
    rest = jnp.zeros((8 - kv, rows.shape[1]), F32)
    return [jnp.concatenate([rows[n * kv : (n + 1) * kv], rest], axis=0) for n in range(3)]


def block_biases(number, per, blocks, b, tokens):
    block = number * per + iota((1, tokens), 1) // BLK
    listed = block == blocks[b, 0]
    for j in range(1, blocks.shape[1]):
        listed = jnp.logical_or(listed, block == blocks[b, j])
    return jnp.where(listed, 0.0, NEG)


def local_kernel(kv, numbers, queries, piece, blocks, gain, q_out, lin_out, grown_out, bias_out, gain_out, q_in, sems):
    copy = pltpu.make_async_copy(queries, q_in, sems.at[0])
    copy.start()
    gain_copy = pltpu.make_async_copy(gain, gain_out, sems.at[1])
    gain_copy.start()
    tokens, heads, width = queries.shape
    rep = heads // kv
    rows = tokens * rep
    per = blocks.shape[0]
    parts = [p.astype(BF16) for p in parts_of(piece, kv)]
    upto = iota((rows, tokens), 1) <= iota((rows, tokens), 0) // rep
    ones = jnp.where(upto, 1.0, 0.0).astype(BF16)
    ahead = jnp.where(iota((tokens, tokens), 0) <= iota((tokens, tokens), 1), 1.0, 0.0).astype(BF16)
    cum_row = mm(parts[0], ahead) + mm(parts[1], ahead) + mm(parts[2], ahead)
    cum_col = mm(ones, parts[0], NT) + mm(ones, parts[1], NT) + mm(ones, parts[2], NT)
    if numbers is not None:
        rows_of = [block_biases(n, per, blocks, b, tokens) for b in range(per) for n in numbers()]
        for r, row in enumerate(rows_of):
            bias_out[r : r + 1, :] = row
    copy.wait()
    qf = q_in[...].astype(F32)
    for g in range(kv):
        q = qf[:, g * rep : (g + 1) * rep, :].reshape(rows, width).astype(BF16)
        q_out[g] = q
        k = piece[g * tokens : (g + 1) * tokens, :]
        v = piece[(kv + g) * tokens : (kv + g + 1) * tokens, :]
        cum = jnp.broadcast_to(cum_col[:, g : g + 1], (rows, tokens))
        grown_out[g] = jnp.exp(cum)
        weight = jnp.where(upto, jnp.exp(jnp.minimum(cum - cum_row[g : g + 1, :], 0.0)), 0.0)
        hi, lo = halves(mm(q, k, NT) * weight)
        lin_out[g] = mm(hi, v) + mm(lo, v)
    gain_copy.wait()


def attend(kv, b, per, queries, pieces, biases, own, scores, out):
    _, rows, width = queries.shape
    part = rows // per
    factor = width**-0.5 * 1.4426950408889634
    tokens = scores.shape[1] // len(pieces)
    for g in range(kv):
        q = queries[g, b * part : (b + 1) * part, :]
        top = None
        for i, piece in enumerate(pieces):
            s = mm(q, piece[g * tokens : (g + 1) * tokens, :], NT) + biases[i]
            mask = own(i, (part, tokens))
            if mask is not None:
                s = jnp.where(mask, s, NEG)
            scores[:, i * tokens : (i + 1) * tokens] = s
            top = s if top is None else jnp.maximum(top, s)
        top = jnp.max(top, axis=1, keepdims=True)
        total, acc = None, None
        for i, piece in enumerate(pieces):
            e = jnp.exp2((scores[:, i * tokens : (i + 1) * tokens] - top) * factor)
            o = mm(e.astype(BF16), piece[(kv + g) * tokens : (kv + g + 1) * tokens, :])
            total = e if total is None else total + e
            acc = o if acc is None else acc + o
        out[g, b * part : (b + 1) * part, :] = acc / jnp.sum(total, axis=1, keepdims=True)


def suffixes(parts, tokens):
    after = jnp.where(iota((tokens, tokens), 1) > iota((tokens, tokens), 0), 1.0, 0.0).astype(BF16)
    hi, mid, lo = (p.astype(BF16) for p in parts)
    return mm(after, hi, NT) + mm(after, mid, NT) + mm(after, lo, NT)


def totals(parts):
    return jnp.sum(parts[0] + parts[1] + parts[2], axis=1, keepdims=True)


def own_states(kv, piece, suffix, shift):
    tokens = suffix.shape[0]
    result = []
    for g in range(kv):
        w = jnp.exp(jnp.minimum(suffix[:, g : g + 1] + shift[g], 0.0))
        k = piece[g * tokens : (g + 1) * tokens, :]
        hi, lo = halves(piece[(kv + g) * tokens : (kv + g + 1) * tokens, :].astype(F32) * w)
        result.append(mm(k, hi, TN) + mm(k, lo, TN))
    return result


def finish(kv, queries, lin, grown, sparse, gain, state, out):
    _, rows, width = queries.shape
    tokens, heads, _ = out.shape
    rep = heads // kv
    both = []
    for g in range(kv):
        q = queries[g]
        hi, lo = halves(state[g])
        linear = lin[g] + grown[g] * (mm(q, hi) + mm(q, lo))
        mean = jnp.mean(linear * linear, axis=1, keepdims=True)
        normed = (linear * lax.rsqrt(mean + 1e-06)).reshape(tokens, rep, width)
        normed = normed * gain[g * rep : (g + 1) * rep, :][None]
        both.append(normed + sparse[g].reshape(tokens, rep, width))
    out[...] = jnp.concatenate(both, axis=1).astype(BF16)


def column_kernel(kv, slots, ids, queries, blocks, column, out, scores):
    per = blocks.shape[0]
    tokens = per * BLK
    rep = queries.shape[1] // tokens
    here, number = ids()
    for b in range(per):

        def own(i, shape):
            position = here * tokens + b * BLK + iota(shape, 0) // rep
            return number(i) * tokens + iota(shape, 1) <= position

        biases = [block_biases(number(i), per, blocks, b, tokens) for i in range(slots)]
        attend(kv, b, per, queries, [column.at[i] for i in range(slots)], biases, own, scores, out)


def final_kernel(kv, slots, place, queries, lin, grown, sparse, gain, everything, out):
    tokens = out.shape[0]
    width = queries.shape[2]

    def turn(n, carry):
        shift, state = carry
        at, keep = place(n)
        piece = everything.at[at]
        parts = parts_of(piece, kv)
        shifts = [shift[g : g + 1, :] for g in range(kv)]
        more = own_states(kv, piece, suffixes(parts, tokens), shifts)
        state = tuple(s + jnp.where(keep, m, 0.0) for s, m in zip(state, more))
        return shift + jnp.where(keep, totals(parts), 0.0), state

    zero = tuple(jnp.zeros((width, width), F32) for _ in range(kv))
    _, state = lax.fori_loop(0, slots, turn, (jnp.zeros((8, 1), F32), zero))
    finish(kv, queries, lin, grown, sparse, gain, state, out)


def shift_of(i, sums, far):
    shift = jnp.zeros((8, 1), F32)
    for j, total in enumerate(sums):
        if j != i:
            shift = shift + jnp.where(far[j] < far[-1 if i is None else i], total, 0.0)
    return shift


def sparse_kernel(kv, n_column, per, distance, queries, biases, *refs):
    *pieces, out, states, factor, scores = refs
    column = pieces[:n_column]
    tokens = per * BLK
    rep = queries.shape[1] // tokens
    far = distance()
    parts = [parts_of(p, kv) for p in pieces[1:]]
    suffix = suffixes([jnp.concatenate(p, axis=0) for p in zip(*parts)], tokens)
    sums = [totals(p) for p in parts]
    near, beyond = [0.0] * kv, [0.0] * kv
    for i, piece in enumerate(pieces[1:]):
        shift = shift_of(i, sums, far)
        more = own_states(kv, piece, suffix[:, 8 * i : 8 * i + 8], [shift[g : g + 1, :] for g in range(kv)])
        closer = far[i] < far[-1]
        behind = jnp.logical_and(far[i] > far[-1], far[i] < NEVER)
        for g in range(kv):
            near[g] = near[g] + jnp.where(closer, more[g], 0.0)
            beyond[g] = beyond[g] + jnp.where(behind, more[g], 0.0)
    for g in range(kv):
        states[g], states[kv + g] = near[g], beyond[g]
    factor[...] = jnp.broadcast_to(jnp.exp(shift_of(None, sums, far)), factor.shape)
    for b in range(per):

        def own(i, shape):
            return iota(shape, 1) <= b * BLK + iota(shape, 0) // rep if i == 0 else None

        rows = [biases[b * n_column + i : b * n_column + i + 1, :] for i in range(n_column)]
        attend(kv, b, per, queries, column, rows, own, scores, out)


def last_kernel(kv, distance, queries, lin, grown, sparse, gain, states, factor, last, out):
    parts = parts_of(last, kv)
    total = jnp.exp(totals(parts))
    keep = distance()[-1] < NEVER
    more = own_states(kv, last, suffixes(parts, out.shape[0]), [0.0] * kv)
    state = []
    for g in range(kv):
        mine = jnp.where(keep, factor[g : g + 1, :] * more[g], 0.0)
        state.append(states[g] + jnp.where(keep, total[g : g + 1, :] * states[kv + g], 0.0) + mine)
    finish(kv, queries, lin, grown, sparse, gain, state, out)


def where_am_i():
    return lax.axis_index("seq"), lax.axis_index("inner")


def pick(table, at):
    value = jnp.int32(table[0])
    for n in range(1, len(table)):
        value = jnp.where(at == n, table[n], value)
    return value


def in_hbm(x):
    return pltpu.with_memory_space_constraint(x, pltpu.HBM)


def shards(queries, keys, values, log_decay, gain, block_list):
    tokens, heads, width = queries.shape
    kv = keys.shape[1]
    rows = tokens * (heads // kv)
    per = tokens // BLK
    n_seq, n_inner = lax.axis_size("seq"), lax.axis_size("inner")
    shape = jax.ShapeDtypeStruct

    def call(kernel, out_shape, in_specs, scratch, *args, cost=None):
        one = not isinstance(out_shape, tuple)
        return pl.pallas_call(
            kernel,
            out_shape=out_shape,
            in_specs=in_specs,
            out_specs=VMEM if one else tuple(VMEM for _ in out_shape),
            scratch_shapes=scratch,
            compiler_params=PARAMS,
            cost_estimate=cost,
        )(*args)

    piece = call(
        functools.partial(pack_kernel, kv),
        shape((2 * kv * tokens + EXTRA, width), BF16),
        [HBM] * 3,
        [
            pltpu.VMEM((2, kv * tokens, width), BF16),
            pltpu.VMEM((kv, tokens), F32),
            pltpu.VMEM((kv * tokens, width), F32),
            pltpu.SemaphoreType.DMA((3,)),
        ],
        in_hbm(keys.reshape(-1, width)),
        in_hbm(values.reshape(-1, width)),
        in_hbm(log_decay.T),
    )
    few = n_seq == 4 and n_inner == 2

    def numbers():
        z, x = where_am_i()
        found = [z * n_inner + x]
        for table in held:
            other = pick(table, z)
            found.append(jnp.where(other < z, other * n_inner + x, -1))
        return found

    def distance():
        z, x = where_am_i()
        mine, theirs = [], [jnp.where(x == 1, 1, NEVER)]
        for table in held:
            other = pick(table, z)
            mine.append(jnp.where(other < z, (z - other) * n_inner, NEVER))
            theirs.append(jnp.where(other < z, (z - other) * n_inner + jnp.where(x == 1, 1, -1), NEVER))
        return mine + theirs

    if few:
        first, second, third = (
            [(0, 2), (2, 3), (1, 1), (3, 0)],
            [(0, 1), (1, 3), (3, 2), (2, 0)],
            [(1, 2), (2, 3), (0, 0), (3, 1)],
        )
        came = [{b: a for a, b in pairs} for pairs in (first, second, third)]
        held = [[came[0][i] for i in range(4)], [came[1][i] for i in range(4)], [came[0][came[2][i]] for i in range(4)]]

    q, lin, grown, biases, gain = call(
        functools.partial(local_kernel, kv, numbers if few else None),
        (
            shape((kv, rows, width), BF16),
            shape((kv, rows, width), F32),
            shape((kv, rows, tokens), F32),
            shape((8, tokens), F32),
            shape(gain.shape, F32),
        ),
        [HBM, VMEM, SMEM, HBM],
        [pltpu.VMEM(queries.shape, BF16), pltpu.SemaphoreType.DMA((2,))],
        in_hbm(queries),
        piece,
        block_list,
        in_hbm(gain),
        cost=pl.CostEstimate(flops=4 * 10**9, bytes_accessed=4 * 10**6, transcendentals=10**6),
    )
    if few:

        def swap(x):
            return lax.ppermute(x, "inner", [(0, 1), (1, 0)])

        theirs = swap(piece)
        got1 = lax.ppermute(piece, "seq", first)
        got2 = lax.ppermute(piece, "seq", second)
        got1, q, theirs = lax.optimization_barrier((got1, q, theirs))
        got3 = lax.ppermute(got1, "seq", third)
        column = [piece, got1, got2, got3]
        other = [theirs, *(swap(x) for x in column[1:])]

    out_shape = shape((tokens, heads, width), BF16)
    if few:
        sparse, states, factor = call(
            functools.partial(sparse_kernel, kv, n_seq, per, distance),
            (shape((kv, rows, width), F32), shape((2 * kv, width, width), F32), shape((8, width), F32)),
            [VMEM] * (2 + 2 * n_seq - 1),
            [pltpu.VMEM((rows // per, n_seq * tokens), F32)],
            q,
            biases,
            *column,
            *other[:-1],
        )
        return call(
            functools.partial(last_kernel, kv, distance),
            out_shape,
            [VMEM] * 8,
            [],
            q,
            lin,
            grown,
            sparse,
            gain,
            states,
            factor,
            other[-1],
        )

    column = lax.all_gather(piece, "seq")
    everything = lax.all_gather(column, "inner").reshape(n_inner * n_seq, *piece.shape)

    def ids():
        z, x = where_am_i()
        return z * n_inner + x, lambda i: i * n_inner + x

    def place(n):
        z, x = where_am_i()
        p = n_seq * n_inner - 1 - n
        return lax.rem(p, n_inner) * n_seq + lax.div(p, n_inner), p < z * n_inner + x

    sparse = call(
        functools.partial(column_kernel, kv, n_seq, ids),
        shape((kv, rows, width), F32),
        [VMEM, SMEM, VMEM],
        [pltpu.VMEM((rows // per, n_seq * tokens), F32)],
        q,
        block_list,
        column,
    )
    return call(
        functools.partial(final_kernel, kv, n_seq * n_inner, place),
        out_shape,
        [VMEM] * 6,
        [],
        q,
        lin,
        grown,
        sparse,
        gain,
        everything,
    )


def solution(mesh):
    tokens = P(("groups", "seq", "inner"), "head", None)
    return jax.shard_map(
        shards,
        mesh=mesh,
        in_specs=(
            tokens,
            tokens,
            tokens,
            P(("groups", "seq", "inner"), "head"),
            P("head", None),
            P(("groups", "seq", "inner"), None),
        ),
        out_specs=tokens,
        check_vma=False,
    )
```

time: 110 us -> 26.6 us (0.24)
  the two profiles are of different devices: /device:TPU:0 before, /device:TPU:12 now
where the time goes in v2:
time: 26.6 us; the launch traced here: 26.4 us
  starting transfers between devices  12.7 us (48%)
  Pallas kernels  7.83 us (29%)
  waiting for transfers between devices  5.75 us (22%)
    pallas_call x4, Pallas kernels, call(): pl.pallas_call(kernel, out_shape=out_shape, in_specs=in_specs, out_specs=...  7.83 us
    ppermute x4, starting transfers between devices, swap(): return lax.ppermute(x, 'inner', [(0, 1), (1, 0)])  4.18 us
    ppermute x1, starting transfers between devices, shards(): got2 = lax.ppermute(piece, 'seq', second)  4.05 us
    ppermute x4, waiting for transfers between devices, swap(): return lax.ppermute(x, 'inner', [(0, 1), (1, 0)])  3.89 us
    ppermute x1, starting transfers between devices, shards(): got3 = lax.ppermute(got1, 'seq', third)  3.84 us
    ppermute x1, waiting for transfers between devices, shards(): got3 = lax.ppermute(got1, 'seq', third)  1.86 us
    ppermute x1, starting transfers between devices, shards(): got1 = lax.ppermute(piece, 'seq', first)  0.67 us
  transfers between devices with their start and end apart: 7, of which 3 were waited for; matrix products, arithmetic and copies ran while one was open for 0% of the time, Pallas kernels for 19%

profile of v2, /device:TPU:12, one launch (start us, length us, event | category | flops | bytes accessed | tf_op | source)
XLA Modules:
  0.0 26.4 jit_solution(7495332008420696773)
XLA Ops:
  0.0 0.0 copy-start
  0.0 0.9 %shard_map.64.piece.refs_0_ = bf16[528,128]{1,0:T(8,128)(2,1)S(1)} custom-call(bf16[256,128]{1,0:T(8,128)(2,1)} %bitcast.3, bf16[256,128]{1,0:T(8,128)(2,1)} %bitcast.4, f32[2,128]{1,0:T(2,128)} %bitcast.5), custom_call_target="tpu_custom_call" | custom-call | tf_op jit(solution)/shard_map/pallas_call | solution.py:281
  1.0 0.7 %collective-permute-start = (bf16[528,128]{1,0:T(8,128)(2,1)S(1)}, bf16[528,128]{1,0:T(8,128)(2,1)S(1)}, u32[]{:S(2)}, u32[]{:S(2)}) collective-permute-start(bf16[528,128]{1,0:T(8,128)(2,1)S(1)} %shard_map.64.piece.refs_0_), channel_id=1, source_target_pairs={{0,8},{8,12},{4,4},{12,0},{1,9},{9,13},{5,5},{13,1},{2,10},{10,14}... | collective-permute-start | bytes 405512 | tf_op jit(solution)/shard_map/ppermute | solution.py:356
  1.6 1.6 %collective-permute-start.1 = (bf16[528,128]{1,0:T(8,128)(2,1)S(1)}, bf16[528,128]{1,0:T(8,128)(2,1)S(1)}, u32[]{:S(2)}, u32[]{:S(2)}) collective-permute-start(bf16[528,128]{1,0:T(8,128)(2,1)S(1)} %shard_map.64.piece.refs_0_), channel_id=1, source_target_pairs={{0,2},{2,0},{1,3},{3,1},{4,6},{6,4},{5,7},{7,5},{8,10},{10,8},{9,1... | collective-permute-start | bytes 405512 | tf_op jit(solution)/shard_map/ppermute | solution.py:353
  3.2 4.0 %collective-permute-start.2 = (bf16[528,128]{1,0:T(8,128)(2,1)S(1)}, bf16[528,128]{1,0:T(8,128)(2,1)S(1)}, u32[]{:S(2)}, u32[]{:S(2)}) collective-permute-start(bf16[528,128]{1,0:T(8,128)(2,1)S(1)} %shard_map.64.piece.refs_0_), channel_id=1, source_target_pairs={{0,4},{4,12},{12,8},{8,0},{1,5},{5,13},{13,9},{9,1},{2,6},{6,14},{... | collective-permute-start | bytes 405512 | tf_op jit(solution)/shard_map/ppermute | solution.py:357
  7.2 0.0 copy-done
  7.2 2.6 %shard_map.65 = (bf16[2,1024,128]{2,1,0:T(8,128)(2,1)S(1)}, f32[2,1024,128]{2,1,0:T(8,128)S(1)}, f32[2,1024,128]{2,1,0:T(8,128)S(1)}, f32[8,128]{1,0:T(8,128)S(1)}, f32[16,128]{1,0:T(8,128)S(1)}) custom-call(bf16[128,16,128]{2,1,0:T(8,128)(2,1)} %queries.1, bf16[528,128]{1,0:T(8,128)(2,1)S(1)} %shard_map.64.piece.refs_0_, s32[2,16]{1,0:T(2,128)S(1)} %copy-done, ...), custom_call_target="tpu_custom_call" | custom-call | flops 4000000000 | bytes 4000000 | tf_op jit(solution)/shard_map/pallas_call | solution.py:281
  9.8 0.0 collective-permute-done.refs_1_
  9.8 0.0 collective-permute-done.1.refs_4_
  9.9 3.8 %collective-permute-start.3 = (bf16[528,128]{1,0:T(8,128)(2,1)S(1)}, bf16[528,128]{1,0:T(8,128)(2,1)S(1)}, u32[]{:S(2)}, u32[]{:S(2)}) collective-permute-start(bf16[528,128]{1,0:T(8,128)(2,1)S(1)} %collective-permute-done.refs_1_), channel_id=1, source_target_pairs={{4,8},{8,12},{0,0},{12,4},{5,9},{9,13},{1,1},{13,5},{6,10},{10,14}... | collective-permute-start | bytes 405512 | tf_op jit(solution)/shard_map/ppermute | solution.py:359
  13.7 1.6 %collective-permute-start.4 = (bf16[528,128]{1,0:T(8,128)(2,1)S(1)}, bf16[528,128]{1,0:T(8,128)(2,1)S(1)}, u32[]{:S(2)}, u32[]{:S(2)}) collective-permute-start(bf16[528,128]{1,0:T(8,128)(2,1)S(1)} %collective-permute-done.refs_1_), channel_id=1, source_target_pairs={{0,2},{2,0},{1,3},{3,1},{4,6},{6,4},{5,7},{7,5},{8,10},{10,8},{9,1... | collective-permute-start | bytes 405512 | tf_op jit(solution)/shard_map/ppermute | solution.py:353
  15.3 0.0 collective-permute-done.2.refs_2_
  15.3 0.5 %collective-permute-start.5 = (bf16[528,128]{1,0:T(8,128)(2,1)S(1)}, bf16[528,128]{1,0:T(8,128)(2,1)S(1)}, u32[]{:S(2)}, u32[]{:S(2)}) collective-permute-start(bf16[528,128]{1,0:T(8,128)(2,1)S(1)} %collective-permute-done.2.refs_2_), channel_id=1, source_target_pairs={{0,2},{2,0},{1,3},{3,1},{4,6},{6,4},{5,7},{7,5},{8,10},{10,8},{9,1... | collective-permute-start | bytes 405512 | tf_op jit(solution)/shard_map/ppermute | solution.py:353
  15.8 1.9 %collective-permute-done.3.refs_3_ = bf16[528,128]{1,0:T(8,128)(2,1)S(1)} collective-permute-done((bf16[528,128]{1,0:T(8,128)(2,1)S(1)}, bf16[528,128]{1,0:T(8,128)(2,1)S(1)}, u32[]{:S(2)}, u32[]{:S(2)}) %collective-permute-start.3) | collective-permute-done | bytes 135200 | tf_op jit(solution)/shard_map/ppermute | solution.py:359
  17.7 0.5 %collective-permute-start.6 = (bf16[528,128]{1,0:T(8,128)(2,1)S(1)}, bf16[528,128]{1,0:T(8,128)(2,1)S(1)}, u32[]{:S(2)}, u32[]{:S(2)}) collective-permute-start(bf16[528,128]{1,0:T(8,128)(2,1)S(1)} %collective-permute-done.3.refs_3_), channel_id=1, source_target_pairs={{0,2},{2,0},{1,3},{3,1},{4,6},{6,4},{5,7},{7,5},{8,10},{10,8},{9,1... | collective-permute-start | bytes 405512 | tf_op jit(solution)/shard_map/ppermute | solution.py:353
  18.2 2.0 %collective-permute-done.4.refs_5_ = bf16[528,128]{1,0:T(8,128)(2,1)S(1)} collective-permute-done((bf16[528,128]{1,0:T(8,128)(2,1)S(1)}, bf16[528,128]{1,0:T(8,128)(2,1)S(1)}, u32[]{:S(2)}, u32[]{:S(2)}) %collective-permute-start.4) | collective-permute-done | bytes 135200 | tf_op jit(solution)/shard_map/ppermute | solution.py:353
  20.2 1.9 %collective-permute-done.5.refs_6_ = bf16[528,128]{1,0:T(8,128)(2,1)S(1)} collective-permute-done((bf16[528,128]{1,0:T(8,128)(2,1)S(1)}, bf16[528,128]{1,0:T(8,128)(2,1)S(1)}, u32[]{:S(2)}, u32[]{:S(2)}) %collective-permute-start.5) | collective-permute-done | bytes 135200 | tf_op jit(solution)/shard_map/ppermute | solution.py:353
  22.1 2.4 %shard_map.66 = (f32[2,1024,128]{2,1,0:T(8,128)S(1)}, f32[4,128,128]{2,1,0:T(8,128)S(1)}, f32[8,128]{1,0:T(8,128)S(1)}) custom-call(bf16[2,1024,128]{2,1,0:T(8,128)(2,1)S(1)} %get-tuple-element.17.queries, f32[8,128]{1,0:T(8,128)S(1)} %get-tuple-element.20.biases, bf16[528,128]{1,0:T(8,128)(2,1)S(1)} %shard_map.64.piece.refs_0_, ...), custom_call_target="tpu_custom_call" | custom-call | tf_op jit(solution)/shard_map/pallas_call | solution.py:281
  24.5 0.0 collective-permute-done.6.last
  24.5 1.9 %shard_map.67 = bf16[128,16,128]{2,1,0:T(8,128)(2,1)} custom-call(bf16[2,1024,128]{2,1,0:T(8,128)(2,1)S(1)} %get-tuple-element.17.queries, f32[2,1024,128]{2,1,0:T(8,128)S(1)} %get-tuple-element.18.lin, f32[2,1024,128]{2,1,0:T(8,128)S(1)} %get-tuple-element.19.grown, f32[2,1024,128]{2,1,0:T(8,128)S(1)} %get-tuple-element.23.sparse, ...), custom_call_target="tpu_custom_call" | custom-call | tf_op jit(solution)/shard_map/pallas_call | solution.py:281
Async XLA Ops:
  0.0 7.2 %copy-start = (s32[2,16]{1,0:T(2,128)S(1)}, s32[2,16]{1,0:T(2,128)}, u32[]{:S(2)}) copy-start(s32[2,16]{1,0:T(2,128)} %blocks.1) | copy-start | bytes 388
  1.0 8.9 %collective-permute-start = (bf16[528,128]{1,0:T(8,128)(2,1)S(1)}, bf16[528,128]{1,0:T(8,128)(2,1)S(1)}, u32[]{:S(2)}, u32[]{:S(2)}) collective-permute-start(bf16[528,128]{1,0:T(8,128)(2,1)S(1)} %shard_map.64.piece.refs_0_), channel_id=1, source_target_pairs={{0,8},{8,12},{4,4},{12,0},{1,9},{9,13},{5,5},{13,1},{2,10},{10,14}... | collective-permute-start | bytes 405512 | tf_op jit(solution)/shard_map/ppermute | solution.py:356
  1.6 8.2 %collective-permute-start.1 = (bf16[528,128]{1,0:T(8,128)(2,1)S(1)}, bf16[528,128]{1,0:T(8,128)(2,1)S(1)}, u32[]{:S(2)}, u32[]{:S(2)}) collective-permute-start(bf16[528,128]{1,0:T(8,128)(2,1)S(1)} %shard_map.64.piece.refs_0_), channel_id=1, source_target_pairs={{0,2},{2,0},{1,3},{3,1},{4,6},{6,4},{5,7},{7,5},{8,10},{10,8},{9,1... | collective-permute-start | bytes 405512 | tf_op jit(solution)/shard_map/ppermute | solution.py:353
  3.2 12.1 %collective-permute-start.2 = (bf16[528,128]{1,0:T(8,128)(2,1)S(1)}, bf16[528,128]{1,0:T(8,128)(2,1)S(1)}, u32[]{:S(2)}, u32[]{:S(2)}) collective-permute-start(bf16[528,128]{1,0:T(8,128)(2,1)S(1)} %shard_map.64.piece.refs_0_), channel_id=1, source_target_pairs={{0,4},{4,12},{12,8},{8,0},{1,5},{5,13},{13,9},{9,1},{2,6},{6,14},{... | collective-permute-start | bytes 405512 | tf_op jit(solution)/shard_map/ppermute | solution.py:357
  9.9 7.8 %collective-permute-start.3 = (bf16[528,128]{1,0:T(8,128)(2,1)S(1)}, bf16[528,128]{1,0:T(8,128)(2,1)S(1)}, u32[]{:S(2)}, u32[]{:S(2)}) collective-permute-start(bf16[528,128]{1,0:T(8,128)(2,1)S(1)} %collective-permute-done.refs_1_), channel_id=1, source_target_pairs={{4,8},{8,12},{0,0},{12,4},{5,9},{9,13},{1,1},{13,5},{6,10},{10,14}... | collective-permute-start | bytes 405512 | tf_op jit(solution)/shard_map/ppermute | solution.py:359
  13.7 6.5 %collective-permute-start.4 = (bf16[528,128]{1,0:T(8,128)(2,1)S(1)}, bf16[528,128]{1,0:T(8,128)(2,1)S(1)}, u32[]{:S(2)}, u32[]{:S(2)}) collective-permute-start(bf16[528,128]{1,0:T(8,128)(2,1)S(1)} %collective-permute-done.refs_1_), channel_id=1, source_target_pairs={{0,2},{2,0},{1,3},{3,1},{4,6},{6,4},{5,7},{7,5},{8,10},{10,8},{9,1... | collective-permute-start | bytes 405512 | tf_op jit(solution)/shard_map/ppermute | solution.py:353
  15.3 6.8 %collective-permute-start.5 = (bf16[528,128]{1,0:T(8,128)(2,1)S(1)}, bf16[528,128]{1,0:T(8,128)(2,1)S(1)}, u32[]{:S(2)}, u32[]{:S(2)}) collective-permute-start(bf16[528,128]{1,0:T(8,128)(2,1)S(1)} %collective-permute-done.2.refs_2_), channel_id=1, source_target_pairs={{0,2},{2,0},{1,3},{3,1},{4,6},{6,4},{5,7},{7,5},{8,10},{10,8},{9,1... | collective-permute-start | bytes 405512 | tf_op jit(solution)/shard_map/ppermute | solution.py:353
  17.7 6.8 %collective-permute-start.6 = (bf16[528,128]{1,0:T(8,128)(2,1)S(1)}, bf16[528,128]{1,0:T(8,128)(2,1)S(1)}, u32[]{:S(2)}, u32[]{:S(2)}) collective-permute-start(bf16[528,128]{1,0:T(8,128)(2,1)S(1)} %collective-permute-done.3.refs_3_), channel_id=1, source_target_pairs={{0,2},{2,0},{1,3},{3,1},{4,6},{6,4},{5,7},{7,5},{8,10},{10,8},{9,1... | collective-permute-start | bytes 405512 | tf_op jit(solution)/shard_map/ppermute | solution.py:353

commit v3 on v2

--- a/solution.py
+++ b/solution.py
@@ -15,6 +15,8 @@
 TN = (((0,), (0,)), ((), ()))
 NEG = -1e30
 NEVER = 1 << 20
+N_EARLY = 1
+GROUPS = 4
 VMEM = pl.BlockSpec(memory_space=pltpu.VMEM)
 HBM = pl.BlockSpec(memory_space=pltpu.HBM)
 SMEM = pl.BlockSpec(memory_space=pltpu.SMEM)
@@ -149,24 +151,36 @@
         w = jnp.exp(jnp.minimum(suffix[:, g : g + 1] + shift[g], 0.0))
         k = piece[g * tokens : (g + 1) * tokens, :]
         hi, lo = halves(piece[(kv + g) * tokens : (kv + g + 1) * tokens, :].astype(F32) * w)
-        result.append(mm(k, hi, TN) + mm(k, lo, TN))
+        both = mm(k, jnp.concatenate([hi, lo], axis=1), TN)
+        width = hi.shape[1]
+        result.append(both[:, :width] + both[:, width:])
     return result
 
 
-def finish(kv, queries, lin, grown, sparse, gain, state, out):
-    _, rows, width = queries.shape
-    tokens, heads, _ = out.shape
+def finish(kv, queries, lin, grown, sparse, gain, state, out, buffer, sems):
+    tokens, heads, width = out.shape
     rep = heads // kv
-    both = []
-    for g in range(kv):
-        q = queries[g]
-        hi, lo = halves(state[g])
-        linear = lin[g] + grown[g] * (mm(q, hi) + mm(q, lo))
-        mean = jnp.mean(linear * linear, axis=1, keepdims=True)
-        normed = (linear * lax.rsqrt(mean + 1e-06)).reshape(tokens, rep, width)
-        normed = normed * gain[g * rep : (g + 1) * rep, :][None]
-        both.append(normed + sparse[g].reshape(tokens, rep, width))
-    out[...] = jnp.concatenate(both, axis=1).astype(BF16)
+    groups = sems.shape[0]
+    each = tokens // groups
+    split = [jnp.concatenate(halves(s), axis=1) for s in state]
+    copies = []
+    for n in range(groups):
+        rows = slice(n * each * rep, (n + 1) * each * rep)
+        here = slice(n * each, (n + 1) * each)
+        both = []
+        for g in range(kv):
+            q = queries[g, rows, :]
+            inter = mm(q, split[g])
+            linear = lin[g, rows, :] + grown[g, rows, :] * (inter[:, :width] + inter[:, width:])
+            mean = jnp.mean(linear * linear, axis=1, keepdims=True)
+            normed = (linear * lax.rsqrt(mean + 1e-06)).reshape(each, rep, width)
+            normed = normed * gain[g * rep : (g + 1) * rep, :][None]
+            both.append(normed + sparse[g, rows, :].reshape(each, rep, width))
+        buffer[here] = jnp.concatenate(both, axis=1).astype(BF16)
+        copies.append(pltpu.make_async_copy(buffer.at[here], out.at[here], sems.at[n]))
+        copies[-1].start()
+    for c in copies:
+        c.wait()
 
 
 def column_kernel(kv, slots, ids, queries, blocks, column, out, scores):
@@ -184,7 +198,7 @@
         attend(kv, b, per, queries, [column.at[i] for i in range(slots)], biases, own, scores, out)
 
 
-def final_kernel(kv, slots, place, queries, lin, grown, sparse, gain, everything, out):
+def final_kernel(kv, slots, place, queries, lin, grown, sparse, gain, everything, out, buffer, sems):
     tokens = out.shape[0]
     width = queries.shape[2]
 
@@ -200,38 +214,31 @@
 
     zero = tuple(jnp.zeros((width, width), F32) for _ in range(kv))
     _, state = lax.fori_loop(0, slots, turn, (jnp.zeros((8, 1), F32), zero))
-    finish(kv, queries, lin, grown, sparse, gain, state, out)
-
-
-def shift_of(i, sums, far):
-    shift = jnp.zeros((8, 1), F32)
-    for j, total in enumerate(sums):
+    finish(kv, queries, lin, grown, sparse, gain, state, out, buffer, sems)
+
+
+def add_between(shift, i, far, sums):
+    for j, total in sums:
         if j != i:
-            shift = shift + jnp.where(far[j] < far[-1 if i is None else i], total, 0.0)
+            shift = shift + jnp.where(far[j] < far[i], total, 0.0)
     return shift
 
 
 def sparse_kernel(kv, n_column, per, distance, queries, biases, *refs):
-    *pieces, out, states, factor, scores = refs
+    *pieces, out, states, shifts, scores = refs
     column = pieces[:n_column]
     tokens = per * BLK
     rep = queries.shape[1] // tokens
     far = distance()
     parts = [parts_of(p, kv) for p in pieces[1:]]
     suffix = suffixes([jnp.concatenate(p, axis=0) for p in zip(*parts)], tokens)
-    sums = [totals(p) for p in parts]
-    near, beyond = [0.0] * kv, [0.0] * kv
+    sums = [(i, totals(p)) for i, p in enumerate(parts)]
+    for i in range(len(far)):
+        shift = add_between(jnp.zeros((8, 1), F32), i, far, sums)
+        shifts[8 * i : 8 * i + 8, :] = jnp.broadcast_to(shift, (8, shifts.shape[1]))
     for i, piece in enumerate(pieces[1:]):
-        shift = shift_of(i, sums, far)
-        more = own_states(kv, piece, suffix[:, 8 * i : 8 * i + 8], [shift[g : g + 1, :] for g in range(kv)])
-        closer = far[i] < far[-1]
-        behind = jnp.logical_and(far[i] > far[-1], far[i] < NEVER)
-        for g in range(kv):
-            near[g] = near[g] + jnp.where(closer, more[g], 0.0)
-            beyond[g] = beyond[g] + jnp.where(behind, more[g], 0.0)
-    for g in range(kv):
-        states[g], states[kv + g] = near[g], beyond[g]
-    factor[...] = jnp.broadcast_to(jnp.exp(shift_of(None, sums, far)), factor.shape)
+        for g, state in enumerate(own_states(kv, piece, suffix[:, 8 * i : 8 * i + 8], [0.0] * kv)):
+            states[i * kv + g] = state
     for b in range(per):
 
         def own(i, shape):
@@ -241,16 +248,23 @@
         attend(kv, b, per, queries, column, rows, own, scores, out)
 
 
-def last_kernel(kv, distance, queries, lin, grown, sparse, gain, states, factor, last, out):
-    parts = parts_of(last, kv)
-    total = jnp.exp(totals(parts))
-    keep = distance()[-1] < NEVER
-    more = own_states(kv, last, suffixes(parts, out.shape[0]), [0.0] * kv)
-    state = []
-    for g in range(kv):
-        mine = jnp.where(keep, factor[g : g + 1, :] * more[g], 0.0)
-        state.append(states[g] + jnp.where(keep, total[g : g + 1, :] * states[kv + g], 0.0) + mine)
-    finish(kv, queries, lin, grown, sparse, gain, state, out)
+def last_kernel(kv, distance, queries, lin, grown, sparse, gain, states, shifts, *refs):
+    *late, out, buffer, sems = refs
+    far = distance()
+    early = len(far) - len(late)
+    tokens = out.shape[0]
+    parts = [parts_of(p, kv) for p in late]
+    suffix = suffixes([jnp.concatenate(p, axis=0) for p in zip(*parts)], tokens)
+    sums = [(early + n, totals(p)) for n, p in enumerate(parts)]
+    mine = [own_states(kv, p, suffix[:, 8 * n : 8 * n + 8], [0.0] * kv) for n, p in enumerate(late)]
+    state = [0.0] * kv
+    for i in range(len(far)):
+        shift = add_between(shifts[8 * i : 8 * i + 8, :], i, far, sums)
+        factor = jnp.where(far[i] < NEVER, jnp.exp(jnp.minimum(shift, 0.0)), 0.0)
+        for g in range(kv):
+            piece_state = states[i * kv + g] if i < early else mine[i - early][g]
+            state[g] = state[g] + factor[g : g + 1, :] * piece_state
+    finish(kv, queries, lin, grown, sparse, gain, state, out, buffer, sems)
 
 
 def where_am_i():
@@ -276,13 +290,13 @@
     n_seq, n_inner = lax.axis_size("seq"), lax.axis_size("inner")
     shape = jax.ShapeDtypeStruct
 
-    def call(kernel, out_shape, in_specs, scratch, *args, cost=None):
+    def call(kernel, out_shape, in_specs, scratch, *args, cost=None, out_specs=None):
         one = not isinstance(out_shape, tuple)
         return pl.pallas_call(
             kernel,
             out_shape=out_shape,
             in_specs=in_specs,
-            out_specs=VMEM if one else tuple(VMEM for _ in out_shape),
+            out_specs=out_specs or (VMEM if one else tuple(VMEM for _ in out_shape)),
             scratch_shapes=scratch,
             compiler_params=PARAMS,
             cost_estimate=cost,
@@ -325,10 +339,14 @@
         first, second, third = (
             [(0, 2), (2, 3), (1, 1), (3, 0)],
             [(0, 1), (1, 3), (3, 2), (2, 0)],
-            [(1, 2), (2, 3), (0, 0), (3, 1)],
+            [(1, 2), (2, 3)],
         )
         came = [{b: a for a, b in pairs} for pairs in (first, second, third)]
-        held = [[came[0][i] for i in range(4)], [came[1][i] for i in range(4)], [came[0][came[2][i]] for i in range(4)]]
+        held = [
+            [came[0].get(i, n_seq) for i in range(4)],
+            [came[1].get(i, n_seq) for i in range(4)],
+            [came[0].get(came[2].get(i, n_seq), n_seq) for i in range(4)],
+        ]
 
     q, lin, grown, biases, gain = call(
         functools.partial(local_kernel, kv, numbers if few else None),
@@ -356,35 +374,44 @@
         got1 = lax.ppermute(piece, "seq", first)
         got2 = lax.ppermute(piece, "seq", second)
         got1, q, theirs = lax.optimization_barrier((got1, q, theirs))
+        theirs1 = swap(got1)
         got3 = lax.ppermute(got1, "seq", third)
         column = [piece, got1, got2, got3]
-        other = [theirs, *(swap(x) for x in column[1:])]
+        other = [theirs, theirs1, swap(got2), swap(got3)]
 
     out_shape = shape((tokens, heads, width), BF16)
+    write_out = [pltpu.VMEM(out_shape.shape, BF16), pltpu.SemaphoreType.DMA((GROUPS,))]
     if few:
-        sparse, states, factor = call(
+        early = column[1:] + other[:N_EARLY]
+        late = other[N_EARLY:]
+        sparse, states, shifts = call(
             functools.partial(sparse_kernel, kv, n_seq, per, distance),
-            (shape((kv, rows, width), F32), shape((2 * kv, width, width), F32), shape((8, width), F32)),
-            [VMEM] * (2 + 2 * n_seq - 1),
+            (
+                shape((kv, rows, width), F32),
+                shape((len(early) * kv, width, width), F32),
+                shape(((len(early) + len(late)) * 8, width), F32),
+            ),
+            [VMEM] * (3 + len(early)),
             [pltpu.VMEM((rows // per, n_seq * tokens), F32)],
             q,
             biases,
-            *column,
-            *other[:-1],
+            piece,
+            *early,
         )
         return call(
             functools.partial(last_kernel, kv, distance),
             out_shape,
-            [VMEM] * 8,
-            [],
+            [VMEM] * (7 + len(late)),
+            write_out,
             q,
             lin,
             grown,
             sparse,
             gain,
             states,
-            factor,
-            other[-1],
+            shifts,
+            *late,
+            out_specs=HBM,
         )
 
     column = lax.all_gather(piece, "seq")
@@ -412,13 +439,14 @@
         functools.partial(final_kernel, kv, n_seq * n_inner, place),
         out_shape,
         [VMEM] * 6,
-        [],
+        write_out,
         q,
         lin,
         grown,
         sparse,
         gain,
         everything,
+        out_specs=HBM,
     )
 
 

time: 26.6 us -> 25.6 us (0.962)
  waiting for transfers between devices: 5.75 us -> 3.93 us
  starting transfers between devices: 12.7 us -> 13.7 us
    ppermute x1, waiting for transfers between devices: 1.86 us -> 0.42 us  [shards(): got3 = lax.ppermute(got1, 'seq', third)]
    ppermute x4, starting transfers between devices: 4.18 us -> 5.15 us  [swap(): return lax.ppermute(x, 'inner', [(0, 1), (1, 0)])]
    ppermute x4, waiting for transfers between devices: 3.89 us -> 3.5 us  [swap(): return lax.ppermute(x, 'inner', [(0, 1), (1, 0)])]
  transfers between devices with their start and end apart: 7 -> 7, of which waited for: 3 -> 4; matrix products, arithmetic and copies ran while one was open for 0% -> 0% of each run, Pallas kernels for 19% -> 19%
where the time goes in v3:
time: 25.6 us; the launch traced here: 25.4 us
  starting transfers between devices  13.7 us (54%)
  Pallas kernels  7.67 us (30%)
  waiting for transfers between devices  3.93 us (15%)
    pallas_call x4, Pallas kernels, call(): pl.pallas_call(kernel, out_shape=out_shape, in_specs=in_specs, out_specs=...  7.67 us
    ppermute x4, starting transfers between devices, swap(): return lax.ppermute(x, 'inner', [(0, 1), (1, 0)])  5.15 us
    ppermute x1, starting transfers between devices, shards(): got2 = lax.ppermute(piece, 'seq', second)  4.05 us
    ppermute x1, starting transfers between devices, shards(): got3 = lax.ppermute(got1, 'seq', third)  3.85 us
    ppermute x4, waiting for transfers between devices, swap(): return lax.ppermute(x, 'inner', [(0, 1), (1, 0)])  3.5 us
    ppermute x1, starting transfers between devices, shards(): got1 = lax.ppermute(piece, 'seq', first)  0.67 us
  transfers between devices with their start and end apart: 7, of which 4 were waited for; matrix products, arithmetic and copies ran while one was open for 0% of the time, Pallas kernels for 19%

profile of v3, /device:TPU:12, one launch (start us, length us, event | category | flops | bytes accessed | tf_op | source)
XLA Modules:
  0.0 25.4 jit_solution(18051245945326143158)
XLA Ops:
  0.0 0.0 copy-start
  0.0 0.9 %shard_map.64.piece.refs_0_ = bf16[528,128]{1,0:T(8,128)(2,1)S(1)} custom-call(bf16[256,128]{1,0:T(8,128)(2,1)} %bitcast.3, bf16[256,128]{1,0:T(8,128)(2,1)} %bitcast.4, f32[2,128]{1,0:T(2,128)} %bitcast.5), custom_call_target="tpu_custom_call" | custom-call | tf_op jit(solution)/shard_map/pallas_call | solution.py:295
  1.0 0.7 %collective-permute-start = (bf16[528,128]{1,0:T(8,128)(2,1)S(1)}, bf16[528,128]{1,0:T(8,128)(2,1)S(1)}, u32[]{:S(2)}, u32[]{:S(2)}) collective-permute-start(bf16[528,128]{1,0:T(8,128)(2,1)S(1)} %shard_map.64.piece.refs_0_), channel_id=1, source_target_pairs={{0,8},{8,12},{4,4},{12,0},{1,9},{9,13},{5,5},{13,1},{2,10},{10,14}... | collective-permute-start | bytes 405512 | tf_op jit(solution)/shard_map/ppermute | solution.py:374
  1.6 1.6 %collective-permute-start.1 = (bf16[528,128]{1,0:T(8,128)(2,1)S(1)}, bf16[528,128]{1,0:T(8,128)(2,1)S(1)}, u32[]{:S(2)}, u32[]{:S(2)}) collective-permute-start(bf16[528,128]{1,0:T(8,128)(2,1)S(1)} %shard_map.64.piece.refs_0_), channel_id=1, source_target_pairs={{0,2},{2,0},{1,3},{3,1},{4,6},{6,4},{5,7},{7,5},{8,10},{10,8},{9,1... | collective-permute-start | bytes 405512 | tf_op jit(solution)/shard_map/ppermute | solution.py:371
  3.2 4.0 %collective-permute-start.2 = (bf16[528,128]{1,0:T(8,128)(2,1)S(1)}, bf16[528,128]{1,0:T(8,128)(2,1)S(1)}, u32[]{:S(2)}, u32[]{:S(2)}) collective-permute-start(bf16[528,128]{1,0:T(8,128)(2,1)S(1)} %shard_map.64.piece.refs_0_), channel_id=1, source_target_pairs={{0,4},{4,12},{12,8},{8,0},{1,5},{5,13},{13,9},{9,1},{2,6},{6,14},{... | collective-permute-start | bytes 405512 | tf_op jit(solution)/shard_map/ppermute | solution.py:375
  7.2 0.0 copy-done
  7.2 2.6 %shard_map.65 = (bf16[2,1024,128]{2,1,0:T(8,128)(2,1)S(1)}, f32[2,1024,128]{2,1,0:T(8,128)S(1)}, f32[2,1024,128]{2,1,0:T(8,128)S(1)}, f32[8,128]{1,0:T(8,128)S(1)}, f32[16,128]{1,0:T(8,128)S(1)}) custom-call(bf16[128,16,128]{2,1,0:T(8,128)(2,1)} %queries.1, bf16[528,128]{1,0:T(8,128)(2,1)S(1)} %shard_map.64.piece.refs_0_, s32[2,16]{1,0:T(2,128)S(1)} %copy-done, ...), custom_call_target="tpu_custom_call" | custom-call | flops 4000000000 | bytes 4000000 | tf_op jit(solution)/shard_map/pallas_call | solution.py:295
  9.8 0.0 collective-permute-done.refs_1_
  9.8 0.0 collective-permute-done.1.refs_4_
  9.9 3.8 %collective-permute-start.3 = (bf16[528,128]{1,0:T(8,128)(2,1)S(1)}, bf16[528,128]{1,0:T(8,128)(2,1)S(1)}, u32[]{:S(2)}, u32[]{:S(2)}) collective-permute-start(bf16[528,128]{1,0:T(8,128)(2,1)S(1)} %collective-permute-done.refs_1_), channel_id=1, source_target_pairs={{4,8},{8,12},{5,9},{9,13},{6,10},{10,14},{7,11},{11,15},{20,24},{2... | collective-permute-start | bytes 405512 | tf_op jit(solution)/shard_map/ppermute | solution.py:378
  13.7 1.6 %collective-permute-start.4 = (bf16[528,128]{1,0:T(8,128)(2,1)S(1)}, bf16[528,128]{1,0:T(8,128)(2,1)S(1)}, u32[]{:S(2)}, u32[]{:S(2)}) collective-permute-start(bf16[528,128]{1,0:T(8,128)(2,1)S(1)} %collective-permute-done.refs_1_), channel_id=1, source_target_pairs={{0,2},{2,0},{1,3},{3,1},{4,6},{6,4},{5,7},{7,5},{8,10},{10,8},{9,1... | collective-permute-start | bytes 405512 | tf_op jit(solution)/shard_map/ppermute | solution.py:371
  15.3 0.0 collective-permute-done.2.refs_2_
  15.3 0.5 %collective-permute-start.5 = (bf16[528,128]{1,0:T(8,128)(2,1)S(1)}, bf16[528,128]{1,0:T(8,128)(2,1)S(1)}, u32[]{:S(2)}, u32[]{:S(2)}) collective-permute-start(bf16[528,128]{1,0:T(8,128)(2,1)S(1)} %collective-permute-done.2.refs_2_), channel_id=1, source_target_pairs={{0,2},{2,0},{1,3},{3,1},{4,6},{6,4},{5,7},{7,5},{8,10},{10,8},{9,1... | collective-permute-start | bytes 405512 | tf_op jit(solution)/shard_map/ppermute | solution.py:371
  15.8 0.4 %collective-permute-done.3.refs_3_ = bf16[528,128]{1,0:T(8,128)(2,1)S(1)} collective-permute-done((bf16[528,128]{1,0:T(8,128)(2,1)S(1)}, bf16[528,128]{1,0:T(8,128)(2,1)S(1)}, u32[]{:S(2)}, u32[]{:S(2)}) %collective-permute-start.3) | collective-permute-done | bytes 135200 | tf_op jit(solution)/shard_map/ppermute | solution.py:378
  16.2 1.5 %collective-permute-start.6 = (bf16[528,128]{1,0:T(8,128)(2,1)S(1)}, bf16[528,128]{1,0:T(8,128)(2,1)S(1)}, u32[]{:S(2)}, u32[]{:S(2)}) collective-permute-start(bf16[528,128]{1,0:T(8,128)(2,1)S(1)} %collective-permute-done.3.refs_3_), channel_id=1, source_target_pairs={{0,2},{2,0},{1,3},{3,1},{4,6},{6,4},{5,7},{7,5},{8,10},{10,8},{9,1... | collective-permute-start | bytes 405512 | tf_op jit(solution)/shard_map/ppermute | solution.py:371
  17.7 2.3 %shard_map.66 = (f32[2,1024,128]{2,1,0:T(8,128)S(1)}, f32[8,128,128]{2,1,0:T(8,128)S(1)}, f32[56,128]{1,0:T(8,128)S(1)}) custom-call(bf16[2,1024,128]{2,1,0:T(8,128)(2,1)S(1)} %get-tuple-element.17.queries, f32[8,128]{1,0:T(8,128)S(1)} %get-tuple-element.20.biases, bf16[528,128]{1,0:T(8,128)(2,1)S(1)} %shard_map.64.piece.refs_0_, ...), custom_call_target="tpu_custom_call" | custom-call | tf_op jit(solution)/shard_map/pallas_call | solution.py:295
  20.0 0.3 %collective-permute-done.4.refs_0_ = bf16[528,128]{1,0:T(8,128)(2,1)S(1)} collective-permute-done((bf16[528,128]{1,0:T(8,128)(2,1)S(1)}, bf16[528,128]{1,0:T(8,128)(2,1)S(1)}, u32[]{:S(2)}, u32[]{:S(2)}) %collective-permute-start.4) | collective-permute-done | bytes 135200 | tf_op jit(solution)/shard_map/ppermute | solution.py:371
  20.3 1.8 %collective-permute-done.5.refs_1_ = bf16[528,128]{1,0:T(8,128)(2,1)S(1)} collective-permute-done((bf16[528,128]{1,0:T(8,128)(2,1)S(1)}, bf16[528,128]{1,0:T(8,128)(2,1)S(1)}, u32[]{:S(2)}, u32[]{:S(2)}) %collective-permute-start.5) | collective-permute-done | bytes 135200 | tf_op jit(solution)/shard_map/ppermute | solution.py:371
  22.1 1.4 %collective-permute-done.6.refs_2_ = bf16[528,128]{1,0:T(8,128)(2,1)S(1)} collective-permute-done((bf16[528,128]{1,0:T(8,128)(2,1)S(1)}, bf16[528,128]{1,0:T(8,128)(2,1)S(1)}, u32[]{:S(2)}, u32[]{:S(2)}) %collective-permute-start.6) | collective-permute-done | bytes 135200 | tf_op jit(solution)/shard_map/ppermute | solution.py:371
  23.5 1.9 %shard_map.67 = bf16[128,16,128]{2,1,0:T(8,128)(2,1)} custom-call(bf16[2,1024,128]{2,1,0:T(8,128)(2,1)S(1)} %get-tuple-element.17.queries, f32[2,1024,128]{2,1,0:T(8,128)S(1)} %get-tuple-element.18.lin, f32[2,1024,128]{2,1,0:T(8,128)S(1)} %get-tuple-element.19.grown, f32[2,1024,128]{2,1,0:T(8,128)S(1)} %get-tuple-element.23.sparse, ...), custom_call_target="tpu_custom_call" | custom-call | tf_op jit(solution)/shard_map/pallas_call | solution.py:295
Async XLA Ops:
  0.0 7.2 %copy-start = (s32[2,16]{1,0:T(2,128)S(1)}, s32[2,16]{1,0:T(2,128)}, u32[]{:S(2)}) copy-start(s32[2,16]{1,0:T(2,128)} %blocks.1) | copy-start | bytes 388
  1.0 8.9 %collective-permute-start = (bf16[528,128]{1,0:T(8,128)(2,1)S(1)}, bf16[528,128]{1,0:T(8,128)(2,1)S(1)}, u32[]{:S(2)}, u32[]{:S(2)}) collective-permute-start(bf16[528,128]{1,0:T(8,128)(2,1)S(1)} %shard_map.64.piece.refs_0_), channel_id=1, source_target_pairs={{0,8},{8,12},{4,4},{12,0},{1,9},{9,13},{5,5},{13,1},{2,10},{10,14}... | collective-permute-start | bytes 405512 | tf_op jit(solution)/shard_map/ppermute | solution.py:374
  1.6 8.2 %collective-permute-start.1 = (bf16[528,128]{1,0:T(8,128)(2,1)S(1)}, bf16[528,128]{1,0:T(8,128)(2,1)S(1)}, u32[]{:S(2)}, u32[]{:S(2)}) collective-permute-start(bf16[528,128]{1,0:T(8,128)(2,1)S(1)} %shard_map.64.piece.refs_0_), channel_id=1, source_target_pairs={{0,2},{2,0},{1,3},{3,1},{4,6},{6,4},{5,7},{7,5},{8,10},{10,8},{9,1... | collective-permute-start | bytes 405512 | tf_op jit(solution)/shard_map/ppermute | solution.py:371
  3.2 12.1 %collective-permute-start.2 = (bf16[528,128]{1,0:T(8,128)(2,1)S(1)}, bf16[528,128]{1,0:T(8,128)(2,1)S(1)}, u32[]{:S(2)}, u32[]{:S(2)}) collective-permute-start(bf16[528,128]{1,0:T(8,128)(2,1)S(1)} %shard_map.64.piece.refs_0_), channel_id=1, source_target_pairs={{0,4},{4,12},{12,8},{8,0},{1,5},{5,13},{13,9},{9,1},{2,6},{6,14},{... | collective-permute-start | bytes 405512 | tf_op jit(solution)/shard_map/ppermute | solution.py:375
  9.9 6.4 %collective-permute-start.3 = (bf16[528,128]{1,0:T(8,128)(2,1)S(1)}, bf16[528,128]{1,0:T(8,128)(2,1)S(1)}, u32[]{:S(2)}, u32[]{:S(2)}) collective-permute-start(bf16[528,128]{1,0:T(8,128)(2,1)S(1)} %collective-permute-done.refs_1_), channel_id=1, source_target_pairs={{4,8},{8,12},{5,9},{9,13},{6,10},{10,14},{7,11},{11,15},{20,24},{2... | collective-permute-start | bytes 405512 | tf_op jit(solution)/shard_map/ppermute | solution.py:378
  13.7 6.6 %collective-permute-start.4 = (bf16[528,128]{1,0:T(8,128)(2,1)S(1)}, bf16[528,128]{1,0:T(8,128)(2,1)S(1)}, u32[]{:S(2)}, u32[]{:S(2)}) collective-permute-start(bf16[528,128]{1,0:T(8,128)(2,1)S(1)} %collective-permute-done.refs_1_), channel_id=1, source_target_pairs={{0,2},{2,0},{1,3},{3,1},{4,6},{6,4},{5,7},{7,5},{8,10},{10,8},{9,1... | collective-permute-start | bytes 405512 | tf_op jit(solution)/shard_map/ppermute | solution.py:371
  15.3 6.8 %collective-permute-start.5 = (bf16[528,128]{1,0:T(8,128)(2,1)S(1)}, bf16[528,128]{1,0:T(8,128)(2,1)S(1)}, u32[]{:S(2)}, u32[]{:S(2)}) collective-permute-start(bf16[528,128]{1,0:T(8,128)(2,1)S(1)} %collective-permute-done.2.refs_2_), channel_id=1, source_target_pairs={{0,2},{2,0},{1,3},{3,1},{4,6},{6,4},{5,7},{7,5},{8,10},{10,8},{9,1... | collective-permute-start | bytes 405512 | tf_op jit(solution)/shard_map/ppermute | solution.py:371
  16.2 7.3 %collective-permute-start.6 = (bf16[528,128]{1,0:T(8,128)(2,1)S(1)}, bf16[528,128]{1,0:T(8,128)(2,1)S(1)}, u32[]{:S(2)}, u32[]{:S(2)}) collective-permute-start(bf16[528,128]{1,0:T(8,128)(2,1)S(1)} %collective-permute-done.3.refs_3_), channel_id=1, source_target_pairs={{0,2},{2,0},{1,3},{3,1},{4,6},{6,4},{5,7},{7,5},{8,10},{10,8},{9,1... | collective-permute-start | bytes 405512 | tf_op jit(solution)/shard_map/ppermute | solution.py:371

commit v4 on v3

--- a/solution.py
+++ b/solution.py
@@ -104,8 +104,8 @@
         cum = jnp.broadcast_to(cum_col[:, g : g + 1], (rows, tokens))
         grown_out[g] = jnp.exp(cum)
         weight = jnp.where(upto, jnp.exp(jnp.minimum(cum - cum_row[g : g + 1, :], 0.0)), 0.0)
-        hi, lo = halves(mm(q, k, NT) * weight)
-        lin_out[g] = mm(hi, v) + mm(lo, v)
+        both = jnp.concatenate(halves(mm(q, k, NT) * weight), axis=1)
+        lin_out[g] = mm(both, jnp.concatenate([v, v], axis=0))
     gain_copy.wait()
 
 
@@ -162,7 +162,7 @@
     rep = heads // kv
     groups = sems.shape[0]
     each = tokens // groups
-    split = [jnp.concatenate(halves(s), axis=1) for s in state]
+    split = [jnp.concatenate(halves(s), axis=0) for s in state]
     copies = []
     for n in range(groups):
         rows = slice(n * each * rep, (n + 1) * each * rep)
@@ -170,8 +170,8 @@
         both = []
         for g in range(kv):
             q = queries[g, rows, :]
-            inter = mm(q, split[g])
-            linear = lin[g, rows, :] + grown[g, rows, :] * (inter[:, :width] + inter[:, width:])
+            inter = mm(jnp.concatenate([q, q], axis=1), split[g])
+            linear = lin[g, rows, :] + grown[g, rows, :] * inter
             mean = jnp.mean(linear * linear, axis=1, keepdims=True)
             normed = (linear * lax.rsqrt(mean + 1e-06)).reshape(each, rep, width)
             normed = normed * gain[g * rep : (g + 1) * rep, :][None]
@@ -337,7 +337,7 @@
 
     if few:
         first, second, third = (
-            [(0, 2), (2, 3), (1, 1), (3, 0)],
+            [(0, 2), (2, 3), (1, 1)],
             [(0, 1), (1, 3), (3, 2), (2, 0)],
             [(1, 2), (2, 3)],
         )

time: 25.6 us -> 25.5 us (level)
    ppermute x1, starting transfers between devices: 3.85 us -> 4.75 us  [shards(): got3 = lax.ppermute(got1, 'seq', third)]
    ppermute x1, starting transfers between devices: 4.05 us -> 3.21 us  [shards(): got2 = lax.ppermute(piece, 'seq', second)]
where the time goes in v4:
time: 25.5 us; the launch traced here: 25.3 us
  starting transfers between devices  13.8 us (54%)
  Pallas kernels  7.6 us (30%)
  waiting for transfers between devices  3.88 us (15%)
    pallas_call x4, Pallas kernels, call(): pl.pallas_call(kernel, out_shape=out_shape, in_specs=in_specs, out_specs=...  7.6 us
    ppermute x4, starting transfers between devices, swap(): return lax.ppermute(x, 'inner', [(0, 1), (1, 0)])  5.14 us
    ppermute x1, starting transfers between devices, shards(): got3 = lax.ppermute(got1, 'seq', third)  4.75 us
    ppermute x4, waiting for transfers between devices, swap(): return lax.ppermute(x, 'inner', [(0, 1), (1, 0)])  3.44 us
    ppermute x1, starting transfers between devices, shards(): got2 = lax.ppermute(piece, 'seq', second)  3.21 us
    ppermute x1, starting transfers between devices, shards(): got1 = lax.ppermute(piece, 'seq', first)  0.67 us
  transfers between devices with their start and end apart: 7, of which 4 were waited for; matrix products, arithmetic and copies ran while one was open for 0% of the time, Pallas kernels for 19%

profile of v4, /device:TPU:12, one launch (start us, length us, event | category | flops | bytes accessed | tf_op | source)
XLA Modules:
  0.0 25.3 jit_solution(11420044808004022805)
XLA Ops:
  0.0 0.0 copy-start
  0.0 0.9 %shard_map.64.piece.refs_0_ = bf16[528,128]{1,0:T(8,128)(2,1)S(1)} custom-call(bf16[256,128]{1,0:T(8,128)(2,1)} %bitcast.3, bf16[256,128]{1,0:T(8,128)(2,1)} %bitcast.4, f32[2,128]{1,0:T(2,128)} %bitcast.5), custom_call_target="tpu_custom_call" | custom-call | tf_op jit(solution)/shard_map/pallas_call | solution.py:295
  1.0 0.7 %collective-permute-start = (bf16[528,128]{1,0:T(8,128)(2,1)S(1)}, bf16[528,128]{1,0:T(8,128)(2,1)S(1)}, u32[]{:S(2)}, u32[]{:S(2)}) collective-permute-start(bf16[528,128]{1,0:T(8,128)(2,1)S(1)} %shard_map.64.piece.refs_0_), channel_id=1, source_target_pairs={{0,8},{8,12},{4,4},{1,9},{9,13},{5,5},{2,10},{10,14},{6,6},{3,11},... | collective-permute-start | bytes 405512 | tf_op jit(solution)/shard_map/ppermute | solution.py:374
  1.6 1.6 %collective-permute-start.1 = (bf16[528,128]{1,0:T(8,128)(2,1)S(1)}, bf16[528,128]{1,0:T(8,128)(2,1)S(1)}, u32[]{:S(2)}, u32[]{:S(2)}) collective-permute-start(bf16[528,128]{1,0:T(8,128)(2,1)S(1)} %shard_map.64.piece.refs_0_), channel_id=1, source_target_pairs={{0,2},{2,0},{1,3},{3,1},{4,6},{6,4},{5,7},{7,5},{8,10},{10,8},{9,1... | collective-permute-start | bytes 405512 | tf_op jit(solution)/shard_map/ppermute | solution.py:371
  3.2 3.2 %collective-permute-start.2 = (bf16[528,128]{1,0:T(8,128)(2,1)S(1)}, bf16[528,128]{1,0:T(8,128)(2,1)S(1)}, u32[]{:S(2)}, u32[]{:S(2)}) collective-permute-start(bf16[528,128]{1,0:T(8,128)(2,1)S(1)} %shard_map.64.piece.refs_0_), channel_id=1, source_target_pairs={{0,4},{4,12},{12,8},{8,0},{1,5},{5,13},{13,9},{9,1},{2,6},{6,14},{... | collective-permute-start | bytes 405512 | tf_op jit(solution)/shard_map/ppermute | solution.py:375
  6.4 0.0 copy-done
  6.4 2.5 %shard_map.65 = (bf16[2,1024,128]{2,1,0:T(8,128)(2,1)S(1)}, f32[2,1024,128]{2,1,0:T(8,128)S(1)}, f32[2,1024,128]{2,1,0:T(8,128)S(1)}, f32[8,128]{1,0:T(8,128)S(1)}, f32[16,128]{1,0:T(8,128)S(1)}) custom-call(bf16[128,16,128]{2,1,0:T(8,128)(2,1)} %queries.1, bf16[528,128]{1,0:T(8,128)(2,1)S(1)} %shard_map.64.piece.refs_0_, s32[2,16]{1,0:T(2,128)S(1)} %copy-done, ...), custom_call_target="tpu_custom_call" | custom-call | flops 4000000000 | bytes 4000000 | tf_op jit(solution)/shard_map/pallas_call | solution.py:295
  8.9 0.0 collective-permute-done.refs_1_
  8.9 0.0 collective-permute-done.1.refs_4_
  9.0 4.7 %collective-permute-start.3 = (bf16[528,128]{1,0:T(8,128)(2,1)S(1)}, bf16[528,128]{1,0:T(8,128)(2,1)S(1)}, u32[]{:S(2)}, u32[]{:S(2)}) collective-permute-start(bf16[528,128]{1,0:T(8,128)(2,1)S(1)} %collective-permute-done.refs_1_), channel_id=1, source_target_pairs={{4,8},{8,12},{5,9},{9,13},{6,10},{10,14},{7,11},{11,15},{20,24},{2... | collective-permute-start | bytes 405512 | tf_op jit(solution)/shard_map/ppermute | solution.py:378
  13.7 1.6 %collective-permute-start.4 = (bf16[528,128]{1,0:T(8,128)(2,1)S(1)}, bf16[528,128]{1,0:T(8,128)(2,1)S(1)}, u32[]{:S(2)}, u32[]{:S(2)}) collective-permute-start(bf16[528,128]{1,0:T(8,128)(2,1)S(1)} %collective-permute-done.refs_1_), channel_id=1, source_target_pairs={{0,2},{2,0},{1,3},{3,1},{4,6},{6,4},{5,7},{7,5},{8,10},{10,8},{9,1... | collective-permute-start | bytes 405512 | tf_op jit(solution)/shard_map/ppermute | solution.py:371
  15.3 0.0 collective-permute-done.2.refs_2_
  15.3 0.5 %collective-permute-start.5 = (bf16[528,128]{1,0:T(8,128)(2,1)S(1)}, bf16[528,128]{1,0:T(8,128)(2,1)S(1)}, u32[]{:S(2)}, u32[]{:S(2)}) collective-permute-start(bf16[528,128]{1,0:T(8,128)(2,1)S(1)} %collective-permute-done.2.refs_2_), channel_id=1, source_target_pairs={{0,2},{2,0},{1,3},{3,1},{4,6},{6,4},{5,7},{7,5},{8,10},{10,8},{9,1... | collective-permute-start | bytes 405512 | tf_op jit(solution)/shard_map/ppermute | solution.py:371
  15.8 0.4 %collective-permute-done.3.refs_3_ = bf16[528,128]{1,0:T(8,128)(2,1)S(1)} collective-permute-done((bf16[528,128]{1,0:T(8,128)(2,1)S(1)}, bf16[528,128]{1,0:T(8,128)(2,1)S(1)}, u32[]{:S(2)}, u32[]{:S(2)}) %collective-permute-start.3) | collective-permute-done | bytes 135200 | tf_op jit(solution)/shard_map/ppermute | solution.py:378
  16.2 1.5 %collective-permute-start.6 = (bf16[528,128]{1,0:T(8,128)(2,1)S(1)}, bf16[528,128]{1,0:T(8,128)(2,1)S(1)}, u32[]{:S(2)}, u32[]{:S(2)}) collective-permute-start(bf16[528,128]{1,0:T(8,128)(2,1)S(1)} %collective-permute-done.3.refs_3_), channel_id=1, source_target_pairs={{0,2},{2,0},{1,3},{3,1},{4,6},{6,4},{5,7},{7,5},{8,10},{10,8},{9,1... | collective-permute-start | bytes 405512 | tf_op jit(solution)/shard_map/ppermute | solution.py:371
  17.7 2.3 %shard_map.66 = (f32[2,1024,128]{2,1,0:T(8,128)S(1)}, f32[8,128,128]{2,1,0:T(8,128)S(1)}, f32[56,128]{1,0:T(8,128)S(1)}) custom-call(bf16[2,1024,128]{2,1,0:T(8,128)(2,1)S(1)} %get-tuple-element.17.queries, f32[8,128]{1,0:T(8,128)S(1)} %get-tuple-element.20.biases, bf16[528,128]{1,0:T(8,128)(2,1)S(1)} %shard_map.64.piece.refs_0_, ...), custom_call_target="tpu_custom_call" | custom-call | tf_op jit(solution)/shard_map/pallas_call | solution.py:295
  20.0 0.3 %collective-permute-done.4.refs_0_ = bf16[528,128]{1,0:T(8,128)(2,1)S(1)} collective-permute-done((bf16[528,128]{1,0:T(8,128)(2,1)S(1)}, bf16[528,128]{1,0:T(8,128)(2,1)S(1)}, u32[]{:S(2)}, u32[]{:S(2)}) %collective-permute-start.4) | collective-permute-done | bytes 135200 | tf_op jit(solution)/shard_map/ppermute | solution.py:371
  20.3 1.7 %collective-permute-done.5.refs_1_ = bf16[528,128]{1,0:T(8,128)(2,1)S(1)} collective-permute-done((bf16[528,128]{1,0:T(8,128)(2,1)S(1)}, bf16[528,128]{1,0:T(8,128)(2,1)S(1)}, u32[]{:S(2)}, u32[]{:S(2)}) %collective-permute-start.5) | collective-permute-done | bytes 135200 | tf_op jit(solution)/shard_map/ppermute | solution.py:371
  22.0 1.4 %collective-permute-done.6.refs_2_ = bf16[528,128]{1,0:T(8,128)(2,1)S(1)} collective-permute-done((bf16[528,128]{1,0:T(8,128)(2,1)S(1)}, bf16[528,128]{1,0:T(8,128)(2,1)S(1)}, u32[]{:S(2)}, u32[]{:S(2)}) %collective-permute-start.6) | collective-permute-done | bytes 135200 | tf_op jit(solution)/shard_map/ppermute | solution.py:371
  23.5 1.8 %shard_map.67 = bf16[128,16,128]{2,1,0:T(8,128)(2,1)} custom-call(bf16[2,1024,128]{2,1,0:T(8,128)(2,1)S(1)} %get-tuple-element.17.queries, f32[2,1024,128]{2,1,0:T(8,128)S(1)} %get-tuple-element.18.lin, f32[2,1024,128]{2,1,0:T(8,128)S(1)} %get-tuple-element.19.grown, f32[2,1024,128]{2,1,0:T(8,128)S(1)} %get-tuple-element.23.sparse, ...), custom_call_target="tpu_custom_call" | custom-call | tf_op jit(solution)/shard_map/pallas_call | solution.py:295
Async XLA Ops:
  0.0 6.4 %copy-start = (s32[2,16]{1,0:T(2,128)S(1)}, s32[2,16]{1,0:T(2,128)}, u32[]{:S(2)}) copy-start(s32[2,16]{1,0:T(2,128)} %blocks.1) | copy-start | bytes 388
  1.0 8.0 %collective-permute-start = (bf16[528,128]{1,0:T(8,128)(2,1)S(1)}, bf16[528,128]{1,0:T(8,128)(2,1)S(1)}, u32[]{:S(2)}, u32[]{:S(2)}) collective-permute-start(bf16[528,128]{1,0:T(8,128)(2,1)S(1)} %shard_map.64.piece.refs_0_), channel_id=1, source_target_pairs={{0,8},{8,12},{4,4},{1,9},{9,13},{5,5},{2,10},{10,14},{6,6},{3,11},... | collective-permute-start | bytes 405512 | tf_op jit(solution)/shard_map/ppermute | solution.py:374
  1.6 7.3 %collective-permute-start.1 = (bf16[528,128]{1,0:T(8,128)(2,1)S(1)}, bf16[528,128]{1,0:T(8,128)(2,1)S(1)}, u32[]{:S(2)}, u32[]{:S(2)}) collective-permute-start(bf16[528,128]{1,0:T(8,128)(2,1)S(1)} %shard_map.64.piece.refs_0_), channel_id=1, source_target_pairs={{0,2},{2,0},{1,3},{3,1},{4,6},{6,4},{5,7},{7,5},{8,10},{10,8},{9,1... | collective-permute-start | bytes 405512 | tf_op jit(solution)/shard_map/ppermute | solution.py:371
  3.2 12.1 %collective-permute-start.2 = (bf16[528,128]{1,0:T(8,128)(2,1)S(1)}, bf16[528,128]{1,0:T(8,128)(2,1)S(1)}, u32[]{:S(2)}, u32[]{:S(2)}) collective-permute-start(bf16[528,128]{1,0:T(8,128)(2,1)S(1)} %shard_map.64.piece.refs_0_), channel_id=1, source_target_pairs={{0,4},{4,12},{12,8},{8,0},{1,5},{5,13},{13,9},{9,1},{2,6},{6,14},{... | collective-permute-start | bytes 405512 | tf_op jit(solution)/shard_map/ppermute | solution.py:375
  9.0 7.3 %collective-permute-start.3 = (bf16[528,128]{1,0:T(8,128)(2,1)S(1)}, bf16[528,128]{1,0:T(8,128)(2,1)S(1)}, u32[]{:S(2)}, u32[]{:S(2)}) collective-permute-start(bf16[528,128]{1,0:T(8,128)(2,1)S(1)} %collective-permute-done.refs_1_), channel_id=1, source_target_pairs={{4,8},{8,12},{5,9},{9,13},{6,10},{10,14},{7,11},{11,15},{20,24},{2... | collective-permute-start | bytes 405512 | tf_op jit(solution)/shard_map/ppermute | solution.py:378
  13.7 6.6 %collective-permute-start.4 = (bf16[528,128]{1,0:T(8,128)(2,1)S(1)}, bf16[528,128]{1,0:T(8,128)(2,1)S(1)}, u32[]{:S(2)}, u32[]{:S(2)}) collective-permute-start(bf16[528,128]{1,0:T(8,128)(2,1)S(1)} %collective-permute-done.refs_1_), channel_id=1, source_target_pairs={{0,2},{2,0},{1,3},{3,1},{4,6},{6,4},{5,7},{7,5},{8,10},{10,8},{9,1... | collective-permute-start | bytes 405512 | tf_op jit(solution)/shard_map/ppermute | solution.py:371
  15.3 6.7 %collective-permute-start.5 = (bf16[528,128]{1,0:T(8,128)(2,1)S(1)}, bf16[528,128]{1,0:T(8,128)(2,1)S(1)}, u32[]{:S(2)}, u32[]{:S(2)}) collective-permute-start(bf16[528,128]{1,0:T(8,128)(2,1)S(1)} %collective-permute-done.2.refs_2_), channel_id=1, source_target_pairs={{0,2},{2,0},{1,3},{3,1},{4,6},{6,4},{5,7},{7,5},{8,10},{10,8},{9,1... | collective-permute-start | bytes 405512 | tf_op jit(solution)/shard_map/ppermute | solution.py:371
  16.2 7.2 %collective-permute-start.6 = (bf16[528,128]{1,0:T(8,128)(2,1)S(1)}, bf16[528,128]{1,0:T(8,128)(2,1)S(1)}, u32[]{:S(2)}, u32[]{:S(2)}) collective-permute-start(bf16[528,128]{1,0:T(8,128)(2,1)S(1)} %collective-permute-done.3.refs_3_), channel_id=1, source_target_pairs={{0,2},{2,0},{1,3},{3,1},{4,6},{6,4},{5,7},{7,5},{8,10},{10,8},{9,1... | collective-permute-start | bytes 405512 | tf_op jit(solution)/shard_map/ppermute | solution.py:371

commit v5 on v4

--- a/solution.py
+++ b/solution.py
@@ -125,12 +125,13 @@
             scores[:, i * tokens : (i + 1) * tokens] = s
             top = s if top is None else jnp.maximum(top, s)
         top = jnp.max(top, axis=1, keepdims=True)
-        total, acc = None, None
+        total, weights, vals = None, [], []
         for i, piece in enumerate(pieces):
             e = jnp.exp2((scores[:, i * tokens : (i + 1) * tokens] - top) * factor)
-            o = mm(e.astype(BF16), piece[(kv + g) * tokens : (kv + g + 1) * tokens, :])
+            weights.append(e.astype(BF16))
+            vals.append(piece[(kv + g) * tokens : (kv + g + 1) * tokens, :])
             total = e if total is None else total + e
-            acc = o if acc is None else acc + o
+        acc = mm(jnp.concatenate(weights, axis=1), jnp.concatenate(vals, axis=0))
         out[g, b * part : (b + 1) * part, :] = acc / jnp.sum(total, axis=1, keepdims=True)
 
 
@@ -338,7 +339,7 @@
     if few:
         first, second, third = (
             [(0, 2), (2, 3), (1, 1)],
-            [(0, 1), (1, 3), (3, 2), (2, 0)],
+            [(0, 1), (1, 3), (3, 2)],
             [(1, 2), (2, 3)],
         )
         came = [{b: a for a, b in pairs} for pairs in (first, second, third)]

time: 25.5 us -> 26.5 us (1.039)
  the two profiles are of different devices: /device:TPU:12 before, /device:TPU:20 now
where the time goes in v5:
time: 26.5 us; the launch traced here: 26.3 us
  starting transfers between devices  14.6 us (55%)
  Pallas kernels  7.52 us (28%)
  waiting for transfers between devices  4.12 us (16%)
    pallas_call x4, Pallas kernels, call(): pl.pallas_call(kernel, out_shape=out_shape, in_specs=in_specs, out_specs=...  7.52 us
    ppermute x4, starting transfers between devices, swap(): return lax.ppermute(x, 'inner', [(0, 1), (1, 0)])  5.3 us
    ppermute x1, starting transfers between devices, shards(): got3 = lax.ppermute(got1, 'seq', third)  4.55 us
    ppermute x4, waiting for transfers between devices, swap(): return lax.ppermute(x, 'inner', [(0, 1), (1, 0)])  3.67 us
    ppermute x1, starting transfers between devices, shards(): got1 = lax.ppermute(piece, 'seq', first)  3.48 us
    ppermute x1, starting transfers between devices, shards(): got2 = lax.ppermute(piece, 'seq', second)  1.28 us
  transfers between devices with their start and end apart: 7, of which 4 were waited for; matrix products, arithmetic and copies ran while one was open for 0% of the time, Pallas kernels for 18%

profile of v5, /device:TPU:20, one launch (start us, length us, event | category | flops | bytes accessed | tf_op | source)
XLA Modules:
  0.0 26.3 jit_solution(12153055979353873882)
XLA Ops:
  0.0 0.0 copy-start
  0.0 0.9 %shard_map.64.piece.refs_0_ = bf16[528,128]{1,0:T(8,128)(2,1)S(1)} custom-call(bf16[256,128]{1,0:T(8,128)(2,1)} %bitcast.3, bf16[256,128]{1,0:T(8,128)(2,1)} %bitcast.4, f32[2,128]{1,0:T(2,128)} %bitcast.5), custom_call_target="tpu_custom_call" | custom-call | tf_op jit(solution)/shard_map/pallas_call | solution.py:296
  1.0 3.5 %collective-permute-start = (bf16[528,128]{1,0:T(8,128)(2,1)S(1)}, bf16[528,128]{1,0:T(8,128)(2,1)S(1)}, u32[]{:S(2)}, u32[]{:S(2)}) collective-permute-start(bf16[528,128]{1,0:T(8,128)(2,1)S(1)} %shard_map.64.piece.refs_0_), channel_id=1, source_target_pairs={{0,8},{8,12},{4,4},{1,9},{9,13},{5,5},{2,10},{10,14},{6,6},{3,11},... | collective-permute-start | bytes 405512 | tf_op jit(solution)/shard_map/ppermute | solution.py:375
  4.4 1.6 %collective-permute-start.1 = (bf16[528,128]{1,0:T(8,128)(2,1)S(1)}, bf16[528,128]{1,0:T(8,128)(2,1)S(1)}, u32[]{:S(2)}, u32[]{:S(2)}) collective-permute-start(bf16[528,128]{1,0:T(8,128)(2,1)S(1)} %shard_map.64.piece.refs_0_), channel_id=1, source_target_pairs={{0,2},{2,0},{1,3},{3,1},{4,6},{6,4},{5,7},{7,5},{8,10},{10,8},{9,1... | collective-permute-start | bytes 405512 | tf_op jit(solution)/shard_map/ppermute | solution.py:372
  6.0 1.3 %collective-permute-start.2 = (bf16[528,128]{1,0:T(8,128)(2,1)S(1)}, bf16[528,128]{1,0:T(8,128)(2,1)S(1)}, u32[]{:S(2)}, u32[]{:S(2)}) collective-permute-start(bf16[528,128]{1,0:T(8,128)(2,1)S(1)} %shard_map.64.piece.refs_0_), channel_id=1, source_target_pairs={{0,4},{4,12},{12,8},{1,5},{5,13},{13,9},{2,6},{6,14},{14,10},{3,7}... | collective-permute-start | bytes 405512 | tf_op jit(solution)/shard_map/ppermute | solution.py:376
  7.3 0.0 copy-done
  7.3 2.5 %shard_map.65 = (bf16[2,1024,128]{2,1,0:T(8,128)(2,1)S(1)}, f32[2,1024,128]{2,1,0:T(8,128)S(1)}, f32[2,1024,128]{2,1,0:T(8,128)S(1)}, f32[8,128]{1,0:T(8,128)S(1)}, f32[16,128]{1,0:T(8,128)S(1)}) custom-call(bf16[128,16,128]{2,1,0:T(8,128)(2,1)} %queries.1, bf16[528,128]{1,0:T(8,128)(2,1)S(1)} %shard_map.64.piece.refs_0_, s32[2,16]{1,0:T(2,128)S(1)} %copy-done, ...), custom_call_target="tpu_custom_call" | custom-call | flops 4000000000 | bytes 4000000 | tf_op jit(solution)/shard_map/pallas_call | solution.py:296
  9.8 0.0 collective-permute-done.refs_1_
  9.8 0.0 collective-permute-done.1.refs_4_
  9.9 4.6 %collective-permute-start.3 = (bf16[528,128]{1,0:T(8,128)(2,1)S(1)}, bf16[528,128]{1,0:T(8,128)(2,1)S(1)}, u32[]{:S(2)}, u32[]{:S(2)}) collective-permute-start(bf16[528,128]{1,0:T(8,128)(2,1)S(1)} %collective-permute-done.refs_1_), channel_id=1, source_target_pairs={{4,8},{8,12},{5,9},{9,13},{6,10},{10,14},{7,11},{11,15},{20,24},{2... | collective-permute-start | bytes 405512 | tf_op jit(solution)/shard_map/ppermute | solution.py:379
  14.4 0.6 %collective-permute-start.4 = (bf16[528,128]{1,0:T(8,128)(2,1)S(1)}, bf16[528,128]{1,0:T(8,128)(2,1)S(1)}, u32[]{:S(2)}, u32[]{:S(2)}) collective-permute-start(bf16[528,128]{1,0:T(8,128)(2,1)S(1)} %collective-permute-done.refs_1_), channel_id=1, source_target_pairs={{0,2},{2,0},{1,3},{3,1},{4,6},{6,4},{5,7},{7,5},{8,10},{10,8},{9,1... | collective-permute-start | bytes 405512 | tf_op jit(solution)/shard_map/ppermute | solution.py:372
  15.0 0.0 collective-permute-done.2.refs_2_
  15.0 1.5 %collective-permute-start.5 = (bf16[528,128]{1,0:T(8,128)(2,1)S(1)}, bf16[528,128]{1,0:T(8,128)(2,1)S(1)}, u32[]{:S(2)}, u32[]{:S(2)}) collective-permute-start(bf16[528,128]{1,0:T(8,128)(2,1)S(1)} %collective-permute-done.2.refs_2_), channel_id=1, source_target_pairs={{0,2},{2,0},{1,3},{3,1},{4,6},{6,4},{5,7},{7,5},{8,10},{10,8},{9,1... | collective-permute-start | bytes 405512 | tf_op jit(solution)/shard_map/ppermute | solution.py:372
  16.5 0.4 %collective-permute-done.3.refs_3_ = bf16[528,128]{1,0:T(8,128)(2,1)S(1)} collective-permute-done((bf16[528,128]{1,0:T(8,128)(2,1)S(1)}, bf16[528,128]{1,0:T(8,128)(2,1)S(1)}, u32[]{:S(2)}, u32[]{:S(2)}) %collective-permute-start.3) | collective-permute-done | bytes 135200 | tf_op jit(solution)/shard_map/ppermute | solution.py:379
  17.0 1.7 %collective-permute-start.6 = (bf16[528,128]{1,0:T(8,128)(2,1)S(1)}, bf16[528,128]{1,0:T(8,128)(2,1)S(1)}, u32[]{:S(2)}, u32[]{:S(2)}) collective-permute-start(bf16[528,128]{1,0:T(8,128)(2,1)S(1)} %collective-permute-done.3.refs_3_), channel_id=1, source_target_pairs={{0,2},{2,0},{1,3},{3,1},{4,6},{6,4},{5,7},{7,5},{8,10},{10,8},{9,1... | collective-permute-start | bytes 405512 | tf_op jit(solution)/shard_map/ppermute | solution.py:372
  18.6 2.2 %shard_map.66 = (f32[2,1024,128]{2,1,0:T(8,128)S(1)}, f32[8,128,128]{2,1,0:T(8,128)S(1)}, f32[56,128]{1,0:T(8,128)S(1)}) custom-call(bf16[2,1024,128]{2,1,0:T(8,128)(2,1)S(1)} %get-tuple-element.17.queries, f32[8,128]{1,0:T(8,128)S(1)} %get-tuple-element.20.biases, bf16[528,128]{1,0:T(8,128)(2,1)S(1)} %shard_map.64.piece.refs_0_, ...), custom_call_target="tpu_custom_call" | custom-call | tf_op jit(solution)/shard_map/pallas_call | solution.py:296
  20.8 0.2 collective-permute-done.4.refs_0_
  21.0 2.0 %collective-permute-done.5.refs_1_ = bf16[528,128]{1,0:T(8,128)(2,1)S(1)} collective-permute-done((bf16[528,128]{1,0:T(8,128)(2,1)S(1)}, bf16[528,128]{1,0:T(8,128)(2,1)S(1)}, u32[]{:S(2)}, u32[]{:S(2)}) %collective-permute-start.5) | collective-permute-done | bytes 135200 | tf_op jit(solution)/shard_map/ppermute | solution.py:372
  23.0 1.4 %collective-permute-done.6.refs_2_ = bf16[528,128]{1,0:T(8,128)(2,1)S(1)} collective-permute-done((bf16[528,128]{1,0:T(8,128)(2,1)S(1)}, bf16[528,128]{1,0:T(8,128)(2,1)S(1)}, u32[]{:S(2)}, u32[]{:S(2)}) %collective-permute-start.6) | collective-permute-done | bytes 135200 | tf_op jit(solution)/shard_map/ppermute | solution.py:372
  24.5 1.8 %shard_map.67 = bf16[128,16,128]{2,1,0:T(8,128)(2,1)} custom-call(bf16[2,1024,128]{2,1,0:T(8,128)(2,1)S(1)} %get-tuple-element.17.queries, f32[2,1024,128]{2,1,0:T(8,128)S(1)} %get-tuple-element.18.lin, f32[2,1024,128]{2,1,0:T(8,128)S(1)} %get-tuple-element.19.grown, f32[2,1024,128]{2,1,0:T(8,128)S(1)} %get-tuple-element.23.sparse, ...), custom_call_target="tpu_custom_call" | custom-call | tf_op jit(solution)/shard_map/pallas_call | solution.py:296
Async XLA Ops:
  0.0 7.3 %copy-start = (s32[2,16]{1,0:T(2,128)S(1)}, s32[2,16]{1,0:T(2,128)}, u32[]{:S(2)}) copy-start(s32[2,16]{1,0:T(2,128)} %blocks.1) | copy-start | bytes 388
  1.0 8.9 %collective-permute-start = (bf16[528,128]{1,0:T(8,128)(2,1)S(1)}, bf16[528,128]{1,0:T(8,128)(2,1)S(1)}, u32[]{:S(2)}, u32[]{:S(2)}) collective-permute-start(bf16[528,128]{1,0:T(8,128)(2,1)S(1)} %shard_map.64.piece.refs_0_), channel_id=1, source_target_pairs={{0,8},{8,12},{4,4},{1,9},{9,13},{5,5},{2,10},{10,14},{6,6},{3,11},... | collective-permute-start | bytes 405512 | tf_op jit(solution)/shard_map/ppermute | solution.py:375
  4.4 5.4 %collective-permute-start.1 = (bf16[528,128]{1,0:T(8,128)(2,1)S(1)}, bf16[528,128]{1,0:T(8,128)(2,1)S(1)}, u32[]{:S(2)}, u32[]{:S(2)}) collective-permute-start(bf16[528,128]{1,0:T(8,128)(2,1)S(1)} %shard_map.64.piece.refs_0_), channel_id=1, source_target_pairs={{0,2},{2,0},{1,3},{3,1},{4,6},{6,4},{5,7},{7,5},{8,10},{10,8},{9,1... | collective-permute-start | bytes 405512 | tf_op jit(solution)/shard_map/ppermute | solution.py:372
  6.0 9.0 %collective-permute-start.2 = (bf16[528,128]{1,0:T(8,128)(2,1)S(1)}, bf16[528,128]{1,0:T(8,128)(2,1)S(1)}, u32[]{:S(2)}, u32[]{:S(2)}) collective-permute-start(bf16[528,128]{1,0:T(8,128)(2,1)S(1)} %shard_map.64.piece.refs_0_), channel_id=1, source_target_pairs={{0,4},{4,12},{12,8},{1,5},{5,13},{13,9},{2,6},{6,14},{14,10},{3,7}... | collective-permute-start | bytes 405512 | tf_op jit(solution)/shard_map/ppermute | solution.py:376
  9.9 7.1 %collective-permute-start.3 = (bf16[528,128]{1,0:T(8,128)(2,1)S(1)}, bf16[528,128]{1,0:T(8,128)(2,1)S(1)}, u32[]{:S(2)}, u32[]{:S(2)}) collective-permute-start(bf16[528,128]{1,0:T(8,128)(2,1)S(1)} %collective-permute-done.refs_1_), channel_id=1, source_target_pairs={{4,8},{8,12},{5,9},{9,13},{6,10},{10,14},{7,11},{11,15},{20,24},{2... | collective-permute-start | bytes 405512 | tf_op jit(solution)/shard_map/ppermute | solution.py:379
  14.4 6.6 %collective-permute-start.4 = (bf16[528,128]{1,0:T(8,128)(2,1)S(1)}, bf16[528,128]{1,0:T(8,128)(2,1)S(1)}, u32[]{:S(2)}, u32[]{:S(2)}) collective-permute-start(bf16[528,128]{1,0:T(8,128)(2,1)S(1)} %collective-permute-done.refs_1_), channel_id=1, source_target_pairs={{0,2},{2,0},{1,3},{3,1},{4,6},{6,4},{5,7},{7,5},{8,10},{10,8},{9,1... | collective-permute-start | bytes 405512 | tf_op jit(solution)/shard_map/ppermute | solution.py:372
  15.0 8.0 %collective-permute-start.5 = (bf16[528,128]{1,0:T(8,128)(2,1)S(1)}, bf16[528,128]{1,0:T(8,128)(2,1)S(1)}, u32[]{:S(2)}, u32[]{:S(2)}) collective-permute-start(bf16[528,128]{1,0:T(8,128)(2,1)S(1)} %collective-permute-done.2.refs_2_), channel_id=1, source_target_pairs={{0,2},{2,0},{1,3},{3,1},{4,6},{6,4},{5,7},{7,5},{8,10},{10,8},{9,1... | collective-permute-start | bytes 405512 | tf_op jit(solution)/shard_map/ppermute | solution.py:372
  17.0 7.5 %collective-permute-start.6 = (bf16[528,128]{1,0:T(8,128)(2,1)S(1)}, bf16[528,128]{1,0:T(8,128)(2,1)S(1)}, u32[]{:S(2)}, u32[]{:S(2)}) collective-permute-start(bf16[528,128]{1,0:T(8,128)(2,1)S(1)} %collective-permute-done.3.refs_3_), channel_id=1, source_target_pairs={{0,2},{2,0},{1,3},{3,1},{4,6},{6,4},{5,7},{7,5},{8,10},{10,8},{9,1... | collective-permute-start | bytes 405512 | tf_op jit(solution)/shard_map/ppermute | solution.py:372
